TPU v7x, 256 devices: a whole 4x4x8 slice. The times are simulated.
256 devices in a mesh: task: 8 (over y, x_hi), blk: 16 (over z, core), comp: 2 (over x_lo).
Axes of the slice: x: 4 (x_hi: 2, x_lo: 2; x = x_hi * 2 + x_lo), y: 4, z: 8, core: 2. Of those that a mesh axis runs over, the one named last changes fastest.
Arguments:
- query_component_embeddings: bfloat16 [32768, 512], P(('task', 'blk'), 'comp'), parts along dimension 0, may hold values from -13 to 13
- candidate_component_embeddings: bfloat16 [32768, 512], P(('task', 'blk'), 'comp'), parts along dimension 0, may hold values from -1.5 to 1.5
- query_routing_features: bfloat16 [8, 32768], P('comp', ('task', 'blk')), parts along dimension 1, may hold values from -1.5 to 1.5
- candidate_routing_features: bfloat16 [8, 32768], P('comp', ('task', 'blk')), parts along dimension 1, may hold values from -1.5 to 1.5
- own_logit_coefficient: float32 [8], replicated, may hold values from 0.5 to 2.5
- loss_divisor_scale: float32 [8], P('task'), parts along dimension 0, may hold values from 0.1 to 0.2
- target_candidate_index: int32 [32768], P(('task', 'blk')), parts along dimension 0, may hold values from 0 to 4095, each once
Outputs:
- losses: float32 [32768], P(('task', 'blk')), parts along dimension 0
- user_grad: float32 [32768, 512], P(('task', 'blk'), 'comp'), parts along dimension 0
- item_grad: float32 [32768, 512], P(('task', 'blk'), 'comp'), parts along dimension 0
- user_gate_grad: float32 [8, 32768], P('comp', ('task', 'blk')), parts along dimension 1
- item_gate_grad: float32 [8, 32768], P('comp', ('task', 'blk')), parts along dimension 1
There are 8 independent parts, one for each index of `task`. A program takes and returns all parts, laid end to end along the dimension named above; an argument that names none is the same for every part. Nothing has to cross between parts.
Inputs may be any that keep to these rules, and one draw needn't show every extreme that they name: `target_candidate_index`: each item is the positive of exactly one user.
All inputs are finite; a program needn't handle non-finite values.
Results may differ from a plain program's by a relative error of at most 0.0029.
Values may be sent and summed in bfloat16 or wider, within the bound.
A program may use at most 64 MiB of HBM per device.

v0:
```python
import jax
import jax.numpy as jnp
from jax import lax
from jax.sharding import PartitionSpec as P


def passed_along(block, axis, distance):
    devices = range(lax.axis_size(axis))
    route = [((i - distance) % len(devices), i) for i in devices]
    return lax.ppermute(block, axis, route)


def pair_terms(user_split, gate_users, item_split, gate_items, slope_local):
    logits = jnp.einsum("rke,ike->kri", user_split, item_split, preferred_element_type=jnp.float32)
    bent_logit = jnp.tanh(logits)
    weight_matrix = jnp.exp(
        gate_users[:, :, None] + gate_items[:, None, :] + slope_local[:, None, None] * bent_logit
    )
    return (logits, bent_logit, weight_matrix)


def body(
    query_component_embeddings,
    candidate_component_embeddings,
    query_routing_features,
    candidate_routing_features,
    own_logit_coefficient,
    loss_divisor_scale,
    target_candidate_index,
):
    blk_count = lax.axis_size("blk")
    anchor = lax.axis_index("blk")
    normalizer_scale = loss_divisor_scale[0]
    gate_users = query_routing_features.astype(jnp.float32)
    own_comps = query_routing_features.shape[0]
    slope_local = lax.dynamic_slice_in_dim(
        own_logit_coefficient, lax.axis_index("comp") * own_comps, own_comps
    )
    row_count = query_component_embeddings.shape[0]
    local_comps = gate_users.shape[0]
    comp_width = query_component_embeddings.shape[1] // local_comps
    blk_items = candidate_component_embeddings.shape[0]
    user_split = query_component_embeddings.reshape(row_count, local_comps, comp_width)
    column_iota = jnp.arange(blk_items, dtype=jnp.int32)

    def positives(step_index):
        source = (anchor - step_index) % blk_count
        item_ids = source * blk_items + column_iota
        return (target_candidate_index[:, None] == item_ids[None, :]).astype(jnp.float32)

    def forward_step(step_index, item_block, gate_block, scores, denoms, pos_score):
        item_split = item_block.reshape(blk_items, local_comps, comp_width)
        logits, bent_logit, weight_matrix = pair_terms(
            user_split, gate_users, item_split, gate_block.astype(jnp.float32), slope_local
        )
        denom_part = jnp.sum(weight_matrix, axis=0)
        numer_part = jnp.sum(weight_matrix * logits, axis=0)
        denominator, numerator = lax.psum((denom_part, numer_part), "comp")
        pair_score = numerator / denominator
        scores = lax.dynamic_update_index_in_dim(scores, pair_score, step_index, 0)
        denoms = lax.dynamic_update_index_in_dim(denoms, denominator, step_index, 0)
        pos_score = pos_score + jnp.sum(positives(step_index) * pair_score, axis=1)
        return (scores, denoms, pos_score)

    def forward_turn(step_index, loop_state):
        item_block, gate_block, scores, denoms, pos_score = loop_state
        scores, denoms, pos_score = forward_step(
            step_index, item_block, gate_block, scores, denoms, pos_score
        )
        item_block, gate_block = passed_along((item_block, gate_block), "blk", 1)
        return (item_block, gate_block, scores, denoms, pos_score)

    empty_scores = jnp.zeros((blk_count, row_count, blk_items), jnp.float32)
    loop_state = (
        candidate_component_embeddings,
        candidate_routing_features,
        empty_scores,
        empty_scores,
        jnp.zeros((row_count,), jnp.float32),
    )
    item_block, gate_block, scores, denoms, pos_score = lax.fori_loop(
        0, blk_count - 1, forward_turn, loop_state
    )
    scores, denoms, pos_score = forward_step(
        blk_count - 1, item_block, gate_block, scores, denoms, pos_score
    )
    scaled = scores / normalizer_scale
    row_top = jnp.max(scaled, axis=(0, 2))
    log_total = row_top + jnp.log(jnp.sum(jnp.exp(scaled - row_top[None, :, None]), axis=(0, 2)))
    user_loss = log_total - pos_score / normalizer_scale

    def back_step(step_index, item_block, gate_block):
        item_split = item_block.reshape(blk_items, local_comps, comp_width)
        logits, bent_logit, weight_matrix = pair_terms(
            user_split, gate_users, item_split, gate_block.astype(jnp.float32), slope_local
        )
        pair_score = scores[step_index]
        gate_share = weight_matrix / denoms[step_index][None]
        softmax_grad = (
            jnp.exp(pair_score / normalizer_scale - log_total[:, None]) - positives(step_index)
        ) / normalizer_scale
        logit_gap = logits - pair_score[None]
        gate_grad = softmax_grad[None] * gate_share * logit_gap
        logit_grad = (
            softmax_grad[None]
            * gate_share
            * (1.0 + logit_gap * slope_local[:, None, None] * (1.0 - bent_logit * bent_logit))
        ).astype(jnp.bfloat16)
        user_part = jnp.einsum(
            "kri,ike->rke", logit_grad, item_split, preferred_element_type=jnp.float32
        )
        item_part = jnp.einsum(
            "kri,rke->ike", logit_grad, user_split, preferred_element_type=jnp.float32
        )
        return (
            user_part,
            jnp.sum(gate_grad, axis=2),
            item_part.reshape(blk_items, local_comps * comp_width),
            jnp.sum(gate_grad, axis=1),
        )

    def accumulate(step_index, loop_state):
        item_block, gate_block, item_acc, gate_acc, user_acc, user_gate_acc = loop_state
        user_part, user_gate_part, item_part, item_gate_part = back_step(
            step_index, item_block, gate_block
        )
        return (
            item_block,
            gate_block,
            item_acc + item_part,
            gate_acc + item_gate_part,
            user_acc + user_part,
            user_gate_acc + user_gate_part,
        )

    def back_turn(step_index, loop_state):
        item_block, gate_block, item_acc, gate_acc, user_acc, user_gate_acc = accumulate(
            step_index, loop_state
        )
        item_block, gate_block = passed_along((item_block, gate_block), "blk", 1)
        item_acc, gate_acc = passed_along((item_acc, gate_acc), "blk", 1)
        return (item_block, gate_block, item_acc, gate_acc, user_acc, user_gate_acc)

    loop_state = (
        candidate_component_embeddings,
        candidate_routing_features,
        jnp.zeros((blk_items, local_comps * comp_width), jnp.float32),
        jnp.zeros((local_comps, blk_items), jnp.float32),
        jnp.zeros((row_count, local_comps, comp_width), jnp.float32),
        jnp.zeros((local_comps, row_count), jnp.float32),
    )
    loop_state = lax.fori_loop(0, blk_count - 1, back_turn, loop_state)
    item_block, gate_block, item_acc, gate_acc, user_acc, user_gate_acc = accumulate(
        blk_count - 1, loop_state
    )
    item_acc, gate_acc = passed_along((item_acc, gate_acc), "blk", 1)
    user_result = user_acc.reshape(row_count, local_comps * comp_width)
    return (user_loss, user_result, item_acc, user_gate_acc, gate_acc)


def solution(mesh):
    in_specs = (
        P(("task", "blk"), "comp"),
        P(("task", "blk"), "comp"),
        P("comp", ("task", "blk")),
        P("comp", ("task", "blk")),
        P(),
        P("task"),
        P(("task", "blk")),
    )
    out_specs = (
        P(("task", "blk")),
        P(("task", "blk"), "comp"),
        P(("task", "blk"), "comp"),
        P("comp", ("task", "blk")),
        P("comp", ("task", "blk")),
    )
    return jax.shard_map(body, mesh=mesh, in_specs=in_specs, out_specs=out_specs, check_vma=False)
```

profile of v0, /device:TPU:1, one launch (start us, length us, event | category | flops | bytes accessed | tf_op | source)
XLA Modules:
  0.0 975.2 jit_solution(15680623285026776232)
XLA Ops:
  16.9 733.6 %while.50 = (s32[]{:T(128)}, bf16[256,256]{0,1:T(8,128)(2,1)S(1)}, bf16[4,256]{1,0:T(4,128)(2,1)S(1)}, f32[16,256,256]{2,1,0:T(8,128)}, f32[16,256,256]{2,1,0:T(...) while((s32[]{:T(128)}, bf16[256,256]{0,1:T(8,128)(2,1)S(1)}, ...), condition=%wide.region_6.7_spmd.clone, body=%wide.region_0.6_spmd.clone.sunk | while | flops 35456512 | bytes 6325692 | solution.py:81
  18.3 3.0 collective-permute-start
  21.4 44.1 %all-reduce.9.cloned.1.call-done = (f32[256,256]{1,0:T(8,128)}, f32[256,256]{1,0:T(8,128)}) async-done(((f32[256,256]{1,0:T(8,128)}, f32[256,256]{1,0:T(8,128)}), (f32[256,256]{1,0:T(8,128)}, f32[256,256]{1,0:T(8,128)})) %all-reduce.9.cloned.1.call-update) | async-done | bytes 524304 | tf_op jit(solution)/shard_map/while/body/eval_jaxpr/psum | solution.py:58
  71.9 42.4 %all-reduce.9.cloned.1.call-done = (f32[256,256]{1,0:T(8,128)}, f32[256,256]{1,0:T(8,128)}) async-done(((f32[256,256]{1,0:T(8,128)}, f32[256,256]{1,0:T(8,128)}), (f32[256,256]{1,0:T(8,128)}, f32[256,256]{1,0:T(8,128)})) %all-reduce.9.cloned.1.call-update) | async-done | bytes 524304 | tf_op jit(solution)/shard_map/while/body/eval_jaxpr/psum | solution.py:58
  120.8 42.4 %all-reduce.9.cloned.1.call-done = (f32[256,256]{1,0:T(8,128)}, f32[256,256]{1,0:T(8,128)}) async-done(((f32[256,256]{1,0:T(8,128)}, f32[256,256]{1,0:T(8,128)}), (f32[256,256]{1,0:T(8,128)}, f32[256,256]{1,0:T(8,128)})) %all-reduce.9.cloned.1.call-update) | async-done | bytes 524304 | tf_op jit(solution)/shard_map/while/body/eval_jaxpr/psum | solution.py:58
  169.6 42.1 %all-reduce.9.cloned.1.call-done = (f32[256,256]{1,0:T(8,128)}, f32[256,256]{1,0:T(8,128)}) async-done(((f32[256,256]{1,0:T(8,128)}, f32[256,256]{1,0:T(8,128)}), (f32[256,256]{1,0:T(8,128)}, f32[256,256]{1,0:T(8,128)})) %all-reduce.9.cloned.1.call-update) | async-done | bytes 524304 | tf_op jit(solution)/shard_map/while/body/eval_jaxpr/psum | solution.py:58
  218.2 42.1 %all-reduce.9.cloned.1.call-done = (f32[256,256]{1,0:T(8,128)}, f32[256,256]{1,0:T(8,128)}) async-done(((f32[256,256]{1,0:T(8,128)}, f32[256,256]{1,0:T(8,128)}), (f32[256,256]{1,0:T(8,128)}, f32[256,256]{1,0:T(8,128)})) %all-reduce.9.cloned.1.call-update) | async-done | bytes 524304 | tf_op jit(solution)/shard_map/while/body/eval_jaxpr/psum | solution.py:58
  266.8 42.1 %all-reduce.9.cloned.1.call-done = (f32[256,256]{1,0:T(8,128)}, f32[256,256]{1,0:T(8,128)}) async-done(((f32[256,256]{1,0:T(8,128)}, f32[256,256]{1,0:T(8,128)}), (f32[256,256]{1,0:T(8,128)}, f32[256,256]{1,0:T(8,128)})) %all-reduce.9.cloned.1.call-update) | async-done | bytes 524304 | tf_op jit(solution)/shard_map/while/body/eval_jaxpr/psum | solution.py:58
  315.3 42.4 %all-reduce.9.cloned.1.call-done = (f32[256,256]{1,0:T(8,128)}, f32[256,256]{1,0:T(8,128)}) async-done(((f32[256,256]{1,0:T(8,128)}, f32[256,256]{1,0:T(8,128)}), (f32[256,256]{1,0:T(8,128)}, f32[256,256]{1,0:T(8,128)})) %all-reduce.9.cloned.1.call-update) | async-done | bytes 524304 | tf_op jit(solution)/shard_map/while/body/eval_jaxpr/psum | solution.py:58
  364.2 42.4 %all-reduce.9.cloned.1.call-done = (f32[256,256]{1,0:T(8,128)}, f32[256,256]{1,0:T(8,128)}) async-done(((f32[256,256]{1,0:T(8,128)}, f32[256,256]{1,0:T(8,128)}), (f32[256,256]{1,0:T(8,128)}, f32[256,256]{1,0:T(8,128)})) %all-reduce.9.cloned.1.call-update) | async-done | bytes 524304 | tf_op jit(solution)/shard_map/while/body/eval_jaxpr/psum | solution.py:58
  413.1 42.4 %all-reduce.9.cloned.1.call-done = (f32[256,256]{1,0:T(8,128)}, f32[256,256]{1,0:T(8,128)}) async-done(((f32[256,256]{1,0:T(8,128)}, f32[256,256]{1,0:T(8,128)}), (f32[256,256]{1,0:T(8,128)}, f32[256,256]{1,0:T(8,128)})) %all-reduce.9.cloned.1.call-update) | async-done | bytes 524304 | tf_op jit(solution)/shard_map/while/body/eval_jaxpr/psum | solution.py:58
  461.9 42.1 %all-reduce.9.cloned.1.call-done = (f32[256,256]{1,0:T(8,128)}, f32[256,256]{1,0:T(8,128)}) async-done(((f32[256,256]{1,0:T(8,128)}, f32[256,256]{1,0:T(8,128)}), (f32[256,256]{1,0:T(8,128)}, f32[256,256]{1,0:T(8,128)})) %all-reduce.9.cloned.1.call-update) | async-done | bytes 524304 | tf_op jit(solution)/shard_map/while/body/eval_jaxpr/psum | solution.py:58
  510.5 42.4 %all-reduce.9.cloned.1.call-done = (f32[256,256]{1,0:T(8,128)}, f32[256,256]{1,0:T(8,128)}) async-done(((f32[256,256]{1,0:T(8,128)}, f32[256,256]{1,0:T(8,128)}), (f32[256,256]{1,0:T(8,128)}, f32[256,256]{1,0:T(8,128)})) %all-reduce.9.cloned.1.call-update) | async-done | bytes 524304 | tf_op jit(solution)/shard_map/while/body/eval_jaxpr/psum | solution.py:58
  559.4 42.1 %all-reduce.9.cloned.1.call-done = (f32[256,256]{1,0:T(8,128)}, f32[256,256]{1,0:T(8,128)}) async-done(((f32[256,256]{1,0:T(8,128)}, f32[256,256]{1,0:T(8,128)}), (f32[256,256]{1,0:T(8,128)}, f32[256,256]{1,0:T(8,128)})) %all-reduce.9.cloned.1.call-update) | async-done | bytes 524304 | tf_op jit(solution)/shard_map/while/body/eval_jaxpr/psum | solution.py:58
  607.9 42.4 %all-reduce.9.cloned.1.call-done = (f32[256,256]{1,0:T(8,128)}, f32[256,256]{1,0:T(8,128)}) async-done(((f32[256,256]{1,0:T(8,128)}, f32[256,256]{1,0:T(8,128)}), (f32[256,256]{1,0:T(8,128)}, f32[256,256]{1,0:T(8,128)})) %all-reduce.9.cloned.1.call-update) | async-done | bytes 524304 | tf_op jit(solution)/shard_map/while/body/eval_jaxpr/psum | solution.py:58
  656.8 42.1 %all-reduce.9.cloned.1.call-done = (f32[256,256]{1,0:T(8,128)}, f32[256,256]{1,0:T(8,128)}) async-done(((f32[256,256]{1,0:T(8,128)}, f32[256,256]{1,0:T(8,128)}), (f32[256,256]{1,0:T(8,128)}, f32[256,256]{1,0:T(8,128)})) %all-reduce.9.cloned.1.call-update) | async-done | bytes 524304 | tf_op jit(solution)/shard_map/while/body/eval_jaxpr/psum | solution.py:58
  705.4 42.1 %all-reduce.9.cloned.1.call-done = (f32[256,256]{1,0:T(8,128)}, f32[256,256]{1,0:T(8,128)}) async-done(((f32[256,256]{1,0:T(8,128)}, f32[256,256]{1,0:T(8,128)}), (f32[256,256]{1,0:T(8,128)}, f32[256,256]{1,0:T(8,128)})) %all-reduce.9.cloned.1.call-update) | async-done | bytes 524304 | tf_op jit(solution)/shard_map/while/body/eval_jaxpr/psum | solution.py:58
  752.7 42.7 %all-reduce.7.cloned.1.call-done = (f32[256,256]{0,1:T(8,128)}, f32[256,256]{0,1:T(8,128)}) async-done(((f32[256,256]{0,1:T(8,128)}, f32[256,256]{0,1:T(8,128)}), (f32[256,256]{0,1:T(8,128)}, f32[256,256]{0,1:T(8,128)})) %all-reduce.7.cloned.1.call-update) | async-done | bytes 524304 | tf_op jit(solution)/shard_map/psum | solution.py:58
  798.6 2.7 fusion.6
  803.6 155.9 %while.51 = (s32[]{:T(128)}, bf16[256,256]{0,1:T(8,128)(2,1)S(1)}, bf16[4,256]{1,0:T(4,128)(2,1)S(1)}, f32[256,256]{0,1:T(8,128)S(1)}, f32[4,256]{1,0:T(4,128)S(...) while((s32[]{:T(128)}, bf16[256,256]{0,1:T(8,128)(2,1)S(1)}, ...), condition=%wide.region_17.18_spmd.clone, body=%wide.region_14.17_spmd.clone.sunk | while | flops 105449744 | bytes 9779721 | solution.py:152
  810.8 2.7 collective-permute-done.5
  813.6 2.5 collective-permute-start.2
  824.0 2.5 collective-permute-start.2
  829.8 2.5 collective-permute-start.4
  832.9 2.7 collective-permute-done.5
  835.7 2.5 collective-permute-start.2
  843.7 2.7 collective-permute-done.5
  846.4 2.5 collective-permute-start.2
  853.8 2.7 collective-permute-done.5
  856.5 2.5 collective-permute-start.2
  863.8 2.7 collective-permute-done.5
  866.6 2.5 collective-permute-start.2
  873.9 2.7 collective-permute-done.5
  876.7 2.5 collective-permute-start.2
  884.0 2.7 collective-permute-done.5
  886.7 2.5 collective-permute-start.2
  894.1 2.7 collective-permute-done.5
  896.8 2.5 collective-permute-start.2
  906.9 2.5 collective-permute-start.2
  912.7 2.5 collective-permute-start.4
  915.8 2.7 collective-permute-done.5
  918.5 2.5 collective-permute-start.2
  926.6 2.7 collective-permute-done.5
  929.3 2.5 collective-permute-start.2
  936.6 2.7 collective-permute-done.5
  946.7 2.7 collective-permute-done.5
  956.8 2.7 collective-permute-done.5
  960.9 2.5 collective-permute-start.6
  (532 shorter events, 200.1 us)
Async XLA Ops:
  16.9 48.6 %all-reduce.9.cloned.1.call-start = ((), (), s32[]{:S(2)}) async-start(), calls=%async_computation.1 | async-start | bytes 1048576 | tf_op jit(solution)/shard_map/while/body/eval_jaxpr/psum | solution.py:58
  18.3 50.2 %collective-permute-start = (bf16[256,256]{0,1:T(8,128)(2,1)S(1)}, bf16[256,256]{0,1:T(8,128)(2,1)S(1)}, u32[]{:S(2)}, u32[]{:S(2)}) collective-permute-start(bf16[256,256]{0,1:T(8,128)(2,1)S(1)} %copy.47), channel_id=1, source_target_pairs={{30,0},{0,2},{2,4},{4,6},{6,8},{8,10},{10,12},{12,14},{14,16},{16,... | collective-permute-start | bytes 393224 | tf_op jit(solution)/shard_map/while/body/eval_jaxpr/ppermute | solution.py:10
  21.4 47.2 %collective-permute-start.1 = (bf16[4,256]{1,0:T(4,128)(2,1)S(1)}, bf16[4,256]{1,0:T(4,128)(2,1)S(1)}, u32[]{:S(2)}, u32[]{:S(2)}) collective-permute-start(bf16[4,256]{1,0:T(4,128)(2,1)S(1)} %copy.48), channel_id=1, source_target_pairs={{30,0},{0,2},{2,4},{4,6},{6,8},{8,10},{10,12},{12,14},{14,16},{16,... | collective-permute-start | bytes 6152 | tf_op jit(solution)/shard_map/while/body/eval_jaxpr/ppermute | solution.py:10
  68.6 45.8 %all-reduce.9.cloned.1.call-start = ((), (), s32[]{:S(2)}) async-start(), calls=%async_computation.1 | async-start | bytes 1048576 | tf_op jit(solution)/shard_map/while/body/eval_jaxpr/psum | solution.py:58
  70.0 47.4 %collective-permute-start = (bf16[256,256]{0,1:T(8,128)(2,1)S(1)}, bf16[256,256]{0,1:T(8,128)(2,1)S(1)}, u32[]{:S(2)}, u32[]{:S(2)}) collective-permute-start(bf16[256,256]{0,1:T(8,128)(2,1)S(1)} %copy.47), channel_id=1, source_target_pairs={{30,0},{0,2},{2,4},{4,6},{6,8},{8,10},{10,12},{12,14},{14,16},{16,... | collective-permute-start | bytes 393224 | tf_op jit(solution)/shard_map/while/body/eval_jaxpr/ppermute | solution.py:10
  71.9 45.5 %collective-permute-start.1 = (bf16[4,256]{1,0:T(4,128)(2,1)S(1)}, bf16[4,256]{1,0:T(4,128)(2,1)S(1)}, u32[]{:S(2)}, u32[]{:S(2)}) collective-permute-start(bf16[4,256]{1,0:T(4,128)(2,1)S(1)} %copy.48), channel_id=1, source_target_pairs={{30,0},{0,2},{2,4},{4,6},{6,8},{8,10},{10,12},{12,14},{14,16},{16,... | collective-permute-start | bytes 6152 | tf_op jit(solution)/shard_map/while/body/eval_jaxpr/ppermute | solution.py:10
  117.4 45.8 %all-reduce.9.cloned.1.call-start = ((), (), s32[]{:S(2)}) async-start(), calls=%async_computation.1 | async-start | bytes 1048576 | tf_op jit(solution)/shard_map/while/body/eval_jaxpr/psum | solution.py:58
  118.9 47.4 %collective-permute-start = (bf16[256,256]{0,1:T(8,128)(2,1)S(1)}, bf16[256,256]{0,1:T(8,128)(2,1)S(1)}, u32[]{:S(2)}, u32[]{:S(2)}) collective-permute-start(bf16[256,256]{0,1:T(8,128)(2,1)S(1)} %copy.47), channel_id=1, source_target_pairs={{30,0},{0,2},{2,4},{4,6},{6,8},{8,10},{10,12},{12,14},{14,16},{16,... | collective-permute-start | bytes 393224 | tf_op jit(solution)/shard_map/while/body/eval_jaxpr/ppermute | solution.py:10
  120.7 45.5 %collective-permute-start.1 = (bf16[4,256]{1,0:T(4,128)(2,1)S(1)}, bf16[4,256]{1,0:T(4,128)(2,1)S(1)}, u32[]{:S(2)}, u32[]{:S(2)}) collective-permute-start(bf16[4,256]{1,0:T(4,128)(2,1)S(1)} %copy.48), channel_id=1, source_target_pairs={{30,0},{0,2},{2,4},{4,6},{6,8},{8,10},{10,12},{12,14},{14,16},{16,... | collective-permute-start | bytes 6152 | tf_op jit(solution)/shard_map/while/body/eval_jaxpr/ppermute | solution.py:10
  166.3 45.5 %all-reduce.9.cloned.1.call-start = ((), (), s32[]{:S(2)}) async-start(), calls=%async_computation.1 | async-start | bytes 1048576 | tf_op jit(solution)/shard_map/while/body/eval_jaxpr/psum | solution.py:58
  167.7 47.1 %collective-permute-start = (bf16[256,256]{0,1:T(8,128)(2,1)S(1)}, bf16[256,256]{0,1:T(8,128)(2,1)S(1)}, u32[]{:S(2)}, u32[]{:S(2)}) collective-permute-start(bf16[256,256]{0,1:T(8,128)(2,1)S(1)} %copy.47), channel_id=1, source_target_pairs={{30,0},{0,2},{2,4},{4,6},{6,8},{8,10},{10,12},{12,14},{14,16},{16,... | collective-permute-start | bytes 393224 | tf_op jit(solution)/shard_map/while/body/eval_jaxpr/ppermute | solution.py:10
  169.6 45.2 %collective-permute-start.1 = (bf16[4,256]{1,0:T(4,128)(2,1)S(1)}, bf16[4,256]{1,0:T(4,128)(2,1)S(1)}, u32[]{:S(2)}, u32[]{:S(2)}) collective-permute-start(bf16[4,256]{1,0:T(4,128)(2,1)S(1)} %copy.48), channel_id=1, source_target_pairs={{30,0},{0,2},{2,4},{4,6},{6,8},{8,10},{10,12},{12,14},{14,16},{16,... | collective-permute-start | bytes 6152 | tf_op jit(solution)/shard_map/while/body/eval_jaxpr/ppermute | solution.py:10
  214.8 45.5 %all-reduce.9.cloned.1.call-start = ((), (), s32[]{:S(2)}) async-start(), calls=%async_computation.1 | async-start | bytes 1048576 | tf_op jit(solution)/shard_map/while/body/eval_jaxpr/psum | solution.py:58
  216.3 47.1 %collective-permute-start = (bf16[256,256]{0,1:T(8,128)(2,1)S(1)}, bf16[256,256]{0,1:T(8,128)(2,1)S(1)}, u32[]{:S(2)}, u32[]{:S(2)}) collective-permute-start(bf16[256,256]{0,1:T(8,128)(2,1)S(1)} %copy.47), channel_id=1, source_target_pairs={{30,0},{0,2},{2,4},{4,6},{6,8},{8,10},{10,12},{12,14},{14,16},{16,... | collective-permute-start | bytes 393224 | tf_op jit(solution)/shard_map/while/body/eval_jaxpr/ppermute | solution.py:10
  218.2 45.2 %collective-permute-start.1 = (bf16[4,256]{1,0:T(4,128)(2,1)S(1)}, bf16[4,256]{1,0:T(4,128)(2,1)S(1)}, u32[]{:S(2)}, u32[]{:S(2)}) collective-permute-start(bf16[4,256]{1,0:T(4,128)(2,1)S(1)} %copy.48), channel_id=1, source_target_pairs={{30,0},{0,2},{2,4},{4,6},{6,8},{8,10},{10,12},{12,14},{14,16},{16,... | collective-permute-start | bytes 6152 | tf_op jit(solution)/shard_map/while/body/eval_jaxpr/ppermute | solution.py:10
  263.4 45.5 %all-reduce.9.cloned.1.call-start = ((), (), s32[]{:S(2)}) async-start(), calls=%async_computation.1 | async-start | bytes 1048576 | tf_op jit(solution)/shard_map/while/body/eval_jaxpr/psum | solution.py:58
  264.9 47.1 %collective-permute-start = (bf16[256,256]{0,1:T(8,128)(2,1)S(1)}, bf16[256,256]{0,1:T(8,128)(2,1)S(1)}, u32[]{:S(2)}, u32[]{:S(2)}) collective-permute-start(bf16[256,256]{0,1:T(8,128)(2,1)S(1)} %copy.47), channel_id=1, source_target_pairs={{30,0},{0,2},{2,4},{4,6},{6,8},{8,10},{10,12},{12,14},{14,16},{16,... | collective-permute-start | bytes 393224 | tf_op jit(solution)/shard_map/while/body/eval_jaxpr/ppermute | solution.py:10
  266.7 45.2 %collective-permute-start.1 = (bf16[4,256]{1,0:T(4,128)(2,1)S(1)}, bf16[4,256]{1,0:T(4,128)(2,1)S(1)}, u32[]{:S(2)}, u32[]{:S(2)}) collective-permute-start(bf16[4,256]{1,0:T(4,128)(2,1)S(1)} %copy.48), channel_id=1, source_target_pairs={{30,0},{0,2},{2,4},{4,6},{6,8},{8,10},{10,12},{12,14},{14,16},{16,... | collective-permute-start | bytes 6152 | tf_op jit(solution)/shard_map/while/body/eval_jaxpr/ppermute | solution.py:10
  312.0 45.8 %all-reduce.9.cloned.1.call-start = ((), (), s32[]{:S(2)}) async-start(), calls=%async_computation.1 | async-start | bytes 1048576 | tf_op jit(solution)/shard_map/while/body/eval_jaxpr/psum | solution.py:58
  313.4 47.4 %collective-permute-start = (bf16[256,256]{0,1:T(8,128)(2,1)S(1)}, bf16[256,256]{0,1:T(8,128)(2,1)S(1)}, u32[]{:S(2)}, u32[]{:S(2)}) collective-permute-start(bf16[256,256]{0,1:T(8,128)(2,1)S(1)} %copy.47), channel_id=1, source_target_pairs={{30,0},{0,2},{2,4},{4,6},{6,8},{8,10},{10,12},{12,14},{14,16},{16,... | collective-permute-start | bytes 393224 | tf_op jit(solution)/shard_map/while/body/eval_jaxpr/ppermute | solution.py:10
  315.3 45.5 %collective-permute-start.1 = (bf16[4,256]{1,0:T(4,128)(2,1)S(1)}, bf16[4,256]{1,0:T(4,128)(2,1)S(1)}, u32[]{:S(2)}, u32[]{:S(2)}) collective-permute-start(bf16[4,256]{1,0:T(4,128)(2,1)S(1)} %copy.48), channel_id=1, source_target_pairs={{30,0},{0,2},{2,4},{4,6},{6,8},{8,10},{10,12},{12,14},{14,16},{16,... | collective-permute-start | bytes 6152 | tf_op jit(solution)/shard_map/while/body/eval_jaxpr/ppermute | solution.py:10
  360.8 45.8 %all-reduce.9.cloned.1.call-start = ((), (), s32[]{:S(2)}) async-start(), calls=%async_computation.1 | async-start | bytes 1048576 | tf_op jit(solution)/shard_map/while/body/eval_jaxpr/psum | solution.py:58
  362.3 47.4 %collective-permute-start = (bf16[256,256]{0,1:T(8,128)(2,1)S(1)}, bf16[256,256]{0,1:T(8,128)(2,1)S(1)}, u32[]{:S(2)}, u32[]{:S(2)}) collective-permute-start(bf16[256,256]{0,1:T(8,128)(2,1)S(1)} %copy.47), channel_id=1, source_target_pairs={{30,0},{0,2},{2,4},{4,6},{6,8},{8,10},{10,12},{12,14},{14,16},{16,... | collective-permute-start | bytes 393224 | tf_op jit(solution)/shard_map/while/body/eval_jaxpr/ppermute | solution.py:10
  364.2 45.5 %collective-permute-start.1 = (bf16[4,256]{1,0:T(4,128)(2,1)S(1)}, bf16[4,256]{1,0:T(4,128)(2,1)S(1)}, u32[]{:S(2)}, u32[]{:S(2)}) collective-permute-start(bf16[4,256]{1,0:T(4,128)(2,1)S(1)} %copy.48), channel_id=1, source_target_pairs={{30,0},{0,2},{2,4},{4,6},{6,8},{8,10},{10,12},{12,14},{14,16},{16,... | collective-permute-start | bytes 6152 | tf_op jit(solution)/shard_map/while/body/eval_jaxpr/ppermute | solution.py:10
  409.7 45.8 %all-reduce.9.cloned.1.call-start = ((), (), s32[]{:S(2)}) async-start(), calls=%async_computation.1 | async-start | bytes 1048576 | tf_op jit(solution)/shard_map/while/body/eval_jaxpr/psum | solution.py:58
  411.2 47.4 %collective-permute-start = (bf16[256,256]{0,1:T(8,128)(2,1)S(1)}, bf16[256,256]{0,1:T(8,128)(2,1)S(1)}, u32[]{:S(2)}, u32[]{:S(2)}) collective-permute-start(bf16[256,256]{0,1:T(8,128)(2,1)S(1)} %copy.47), channel_id=1, source_target_pairs={{30,0},{0,2},{2,4},{4,6},{6,8},{8,10},{10,12},{12,14},{14,16},{16,... | collective-permute-start | bytes 393224 | tf_op jit(solution)/shard_map/while/body/eval_jaxpr/ppermute | solution.py:10
  413.0 45.6 %collective-permute-start.1 = (bf16[4,256]{1,0:T(4,128)(2,1)S(1)}, bf16[4,256]{1,0:T(4,128)(2,1)S(1)}, u32[]{:S(2)}, u32[]{:S(2)}) collective-permute-start(bf16[4,256]{1,0:T(4,128)(2,1)S(1)} %copy.48), channel_id=1, source_target_pairs={{30,0},{0,2},{2,4},{4,6},{6,8},{8,10},{10,12},{12,14},{14,16},{16,... | collective-permute-start | bytes 6152 | tf_op jit(solution)/shard_map/while/body/eval_jaxpr/ppermute | solution.py:10
  458.6 45.5 %all-reduce.9.cloned.1.call-start = ((), (), s32[]{:S(2)}) async-start(), calls=%async_computation.1 | async-start | bytes 1048576 | tf_op jit(solution)/shard_map/while/body/eval_jaxpr/psum | solution.py:58
  460.1 47.1 %collective-permute-start = (bf16[256,256]{0,1:T(8,128)(2,1)S(1)}, bf16[256,256]{0,1:T(8,128)(2,1)S(1)}, u32[]{:S(2)}, u32[]{:S(2)}) collective-permute-start(bf16[256,256]{0,1:T(8,128)(2,1)S(1)} %copy.47), channel_id=1, source_target_pairs={{30,0},{0,2},{2,4},{4,6},{6,8},{8,10},{10,12},{12,14},{14,16},{16,... | collective-permute-start | bytes 393224 | tf_op jit(solution)/shard_map/while/body/eval_jaxpr/ppermute | solution.py:10
  461.9 45.2 %collective-permute-start.1 = (bf16[4,256]{1,0:T(4,128)(2,1)S(1)}, bf16[4,256]{1,0:T(4,128)(2,1)S(1)}, u32[]{:S(2)}, u32[]{:S(2)}) collective-permute-start(bf16[4,256]{1,0:T(4,128)(2,1)S(1)} %copy.48), channel_id=1, source_target_pairs={{30,0},{0,2},{2,4},{4,6},{6,8},{8,10},{10,12},{12,14},{14,16},{16,... | collective-permute-start | bytes 6152 | tf_op jit(solution)/shard_map/while/body/eval_jaxpr/ppermute | solution.py:10
  507.2 45.8 %all-reduce.9.cloned.1.call-start = ((), (), s32[]{:S(2)}) async-start(), calls=%async_computation.1 | async-start | bytes 1048576 | tf_op jit(solution)/shard_map/while/body/eval_jaxpr/psum | solution.py:58
  508.6 47.4 %collective-permute-start = (bf16[256,256]{0,1:T(8,128)(2,1)S(1)}, bf16[256,256]{0,1:T(8,128)(2,1)S(1)}, u32[]{:S(2)}, u32[]{:S(2)}) collective-permute-start(bf16[256,256]{0,1:T(8,128)(2,1)S(1)} %copy.47), channel_id=1, source_target_pairs={{30,0},{0,2},{2,4},{4,6},{6,8},{8,10},{10,12},{12,14},{14,16},{16,... | collective-permute-start | bytes 393224 | tf_op jit(solution)/shard_map/while/body/eval_jaxpr/ppermute | solution.py:10
  510.5 45.5 %collective-permute-start.1 = (bf16[4,256]{1,0:T(4,128)(2,1)S(1)}, bf16[4,256]{1,0:T(4,128)(2,1)S(1)}, u32[]{:S(2)}, u32[]{:S(2)}) collective-permute-start(bf16[4,256]{1,0:T(4,128)(2,1)S(1)} %copy.48), channel_id=1, source_target_pairs={{30,0},{0,2},{2,4},{4,6},{6,8},{8,10},{10,12},{12,14},{14,16},{16,... | collective-permute-start | bytes 6152 | tf_op jit(solution)/shard_map/while/body/eval_jaxpr/ppermute | solution.py:10
  556.0 45.5 %all-reduce.9.cloned.1.call-start = ((), (), s32[]{:S(2)}) async-start(), calls=%async_computation.1 | async-start | bytes 1048576 | tf_op jit(solution)/shard_map/while/body/eval_jaxpr/psum | solution.py:58
  557.5 47.1 %collective-permute-start = (bf16[256,256]{0,1:T(8,128)(2,1)S(1)}, bf16[256,256]{0,1:T(8,128)(2,1)S(1)}, u32[]{:S(2)}, u32[]{:S(2)}) collective-permute-start(bf16[256,256]{0,1:T(8,128)(2,1)S(1)} %copy.47), channel_id=1, source_target_pairs={{30,0},{0,2},{2,4},{4,6},{6,8},{8,10},{10,12},{12,14},{14,16},{16,... | collective-permute-start | bytes 393224 | tf_op jit(solution)/shard_map/while/body/eval_jaxpr/ppermute | solution.py:10
  559.3 45.2 %collective-permute-start.1 = (bf16[4,256]{1,0:T(4,128)(2,1)S(1)}, bf16[4,256]{1,0:T(4,128)(2,1)S(1)}, u32[]{:S(2)}, u32[]{:S(2)}) collective-permute-start(bf16[4,256]{1,0:T(4,128)(2,1)S(1)} %copy.48), channel_id=1, source_target_pairs={{30,0},{0,2},{2,4},{4,6},{6,8},{8,10},{10,12},{12,14},{14,16},{16,... | collective-permute-start | bytes 6152 | tf_op jit(solution)/shard_map/while/body/eval_jaxpr/ppermute | solution.py:10
  604.6 45.8 %all-reduce.9.cloned.1.call-start = ((), (), s32[]{:S(2)}) async-start(), calls=%async_computation.1 | async-start | bytes 1048576 | tf_op jit(solution)/shard_map/while/body/eval_jaxpr/psum | solution.py:58
  606.0 47.4 %collective-permute-start = (bf16[256,256]{0,1:T(8,128)(2,1)S(1)}, bf16[256,256]{0,1:T(8,128)(2,1)S(1)}, u32[]{:S(2)}, u32[]{:S(2)}) collective-permute-start(bf16[256,256]{0,1:T(8,128)(2,1)S(1)} %copy.47), channel_id=1, source_target_pairs={{30,0},{0,2},{2,4},{4,6},{6,8},{8,10},{10,12},{12,14},{14,16},{16,... | collective-permute-start | bytes 393224 | tf_op jit(solution)/shard_map/while/body/eval_jaxpr/ppermute | solution.py:10
  607.9 45.6 %collective-permute-start.1 = (bf16[4,256]{1,0:T(4,128)(2,1)S(1)}, bf16[4,256]{1,0:T(4,128)(2,1)S(1)}, u32[]{:S(2)}, u32[]{:S(2)}) collective-permute-start(bf16[4,256]{1,0:T(4,128)(2,1)S(1)} %copy.48), channel_id=1, source_target_pairs={{30,0},{0,2},{2,4},{4,6},{6,8},{8,10},{10,12},{12,14},{14,16},{16,... | collective-permute-start | bytes 6152 | tf_op jit(solution)/shard_map/while/body/eval_jaxpr/ppermute | solution.py:10
  653.5 45.5 %all-reduce.9.cloned.1.call-start = ((), (), s32[]{:S(2)}) async-start(), calls=%async_computation.1 | async-start | bytes 1048576 | tf_op jit(solution)/shard_map/while/body/eval_jaxpr/psum | solution.py:58
  654.9 47.1 %collective-permute-start = (bf16[256,256]{0,1:T(8,128)(2,1)S(1)}, bf16[256,256]{0,1:T(8,128)(2,1)S(1)}, u32[]{:S(2)}, u32[]{:S(2)}) collective-permute-start(bf16[256,256]{0,1:T(8,128)(2,1)S(1)} %copy.47), channel_id=1, source_target_pairs={{30,0},{0,2},{2,4},{4,6},{6,8},{8,10},{10,12},{12,14},{14,16},{16,... | collective-permute-start | bytes 393224 | tf_op jit(solution)/shard_map/while/body/eval_jaxpr/ppermute | solution.py:10
  656.8 45.2 %collective-permute-start.1 = (bf16[4,256]{1,0:T(4,128)(2,1)S(1)}, bf16[4,256]{1,0:T(4,128)(2,1)S(1)}, u32[]{:S(2)}, u32[]{:S(2)}) collective-permute-start(bf16[4,256]{1,0:T(4,128)(2,1)S(1)} %copy.48), channel_id=1, source_target_pairs={{30,0},{0,2},{2,4},{4,6},{6,8},{8,10},{10,12},{12,14},{14,16},{16,... | collective-permute-start | bytes 6152 | tf_op jit(solution)/shard_map/while/body/eval_jaxpr/ppermute | solution.py:10
  702.0 45.5 %all-reduce.9.cloned.1.call-start = ((), (), s32[]{:S(2)}) async-start(), calls=%async_computation.1 | async-start | bytes 1048576 | tf_op jit(solution)/shard_map/while/body/eval_jaxpr/psum | solution.py:58
  703.5 47.1 %collective-permute-start = (bf16[256,256]{0,1:T(8,128)(2,1)S(1)}, bf16[256,256]{0,1:T(8,128)(2,1)S(1)}, u32[]{:S(2)}, u32[]{:S(2)}) collective-permute-start(bf16[256,256]{0,1:T(8,128)(2,1)S(1)} %copy.47), channel_id=1, source_target_pairs={{30,0},{0,2},{2,4},{4,6},{6,8},{8,10},{10,12},{12,14},{14,16},{16,... | collective-permute-start | bytes 393224 | tf_op jit(solution)/shard_map/while/body/eval_jaxpr/ppermute | solution.py:10
  705.3 45.2 %collective-permute-start.1 = (bf16[4,256]{1,0:T(4,128)(2,1)S(1)}, bf16[4,256]{1,0:T(4,128)(2,1)S(1)}, u32[]{:S(2)}, u32[]{:S(2)}) collective-permute-start(bf16[4,256]{1,0:T(4,128)(2,1)S(1)} %copy.48), channel_id=1, source_target_pairs={{30,0},{0,2},{2,4},{4,6},{6,8},{8,10},{10,12},{12,14},{14,16},{16,... | collective-permute-start | bytes 6152 | tf_op jit(solution)/shard_map/while/body/eval_jaxpr/ppermute | solution.py:10
  750.6 44.9 %all-reduce.7.cloned.1.call-start = ((), (), s32[]{:S(2)}) async-start(), calls=%async_computation | async-start | bytes 1048576 | tf_op jit(solution)/shard_map/psum | solution.py:58
  824.0 11.6 %collective-permute-start.2 = (bf16[256,256]{0,1:T(8,128)(2,1)S(1)}, bf16[256,256]{0,1:T(8,128)(2,1)S(1)}, u32[]{:S(2)}, u32[]{:S(2)}) collective-permute-start(bf16[256,256]{0,1:T(8,128)(2,1)S(1)} %copy.70), channel_id=1, source_target_pairs={{30,0},{0,2},{2,4},{4,6},{6,8},{8,10},{10,12},{12,14},{14,16},{16,... | collective-permute-start | bytes 393224 | tf_op jit(solution)/shard_map/while/body/eval_jaxpr/ppermute | solution.py:10
  906.9 11.6 %collective-permute-start.2 = (bf16[256,256]{0,1:T(8,128)(2,1)S(1)}, bf16[256,256]{0,1:T(8,128)(2,1)S(1)}, u32[]{:S(2)}, u32[]{:S(2)}) collective-permute-start(bf16[256,256]{0,1:T(8,128)(2,1)S(1)} %copy.70), channel_id=1, source_target_pairs={{30,0},{0,2},{2,4},{4,6},{6,8},{8,10},{10,12},{12,14},{14,16},{16,... | collective-permute-start | bytes 393224 | tf_op jit(solution)/shard_map/while/body/eval_jaxpr/ppermute | solution.py:10
  (64 other events, 358.4 us)
Sparse Core Ops, SparseCore 0:
  21.1 44.2 all-reduce.8
  72.8 41.4 all-reduce.8
  121.7 41.4 all-reduce.8
  170.2 41.4 all-reduce.8
  218.8 41.4 all-reduce.8
  267.3 41.4 all-reduce.8
  316.2 41.4 all-reduce.8
  365.1 41.4 all-reduce.8
  414.0 41.4 all-reduce.8
  462.5 41.4 all-reduce.8
  511.4 41.4 all-reduce.8
  559.9 41.4 all-reduce.8
  608.8 41.4 all-reduce.8
  657.4 41.4 all-reduce.8
  705.9 41.4 all-reduce.8
Sparse Core Ops, SparseCore 1:
  754.2 41.1 all-reduce.6
where the time goes:
time: 979 us; the launch traced here: 975 us
  waiting for transfers between devices  721 us (74%)
  starting transfers between devices  96.1 us (10%)
  other arithmetic  84.6 us (9%)
  matrix products  42.1 us (4%)
  between operations  16 us (2%)
  local copies, waits for them, and re-layouts  13.8 us (1%)
    psum x16, waiting for transfers between devices, forward_step(): denominator, numerator = lax.psum((denom_part, numer_part), 'comp')  679 us
    ppermute x92, starting transfers between devices, passed_along(): return lax.ppermute(block, axis, route)  95.4 us
    ppermute x92, waiting for transfers between devices, passed_along(): return lax.ppermute(block, axis, route)  41.8 us
    dot_general x32, matrix products, pair_terms(): jnp.einsum('rke,ike->kri', user_split, item_split, preferred_element_type...  34.1 us
    dynamic_update_slice x15, other arithmetic, forward_step(): denoms = lax.dynamic_update_index_in_dim(denoms, denominator, step_index, 0)  27.8 us
    mul x15, other arithmetic, back_step(): softmax_grad[None] * gate_share  27.2 us
  transfers between devices with their start and end apart: 108, of which 32 were waited for; matrix products, arithmetic and copies ran while one was open for 10% of the time, Pallas kernels for 0%

commit v1 on v0

v1 whole, which is shorter than its diff:
```python
import jax
import jax.numpy as jnp
from jax import lax
from jax.experimental import pallas as pl
from jax.experimental.pallas import tpu as pltpu
from jax.sharding import PartitionSpec as P

MESH = pl.DeviceIdType.MESH
LOG2E = 1.4426950408889634
F32, BF16 = jnp.float32, jnp.bfloat16
NZ = 8
UB = 256
US = 512
CH = 128
K = 8
ROWS = 16
NT = (((1,), (1,)), ((), ()))


def kernel(
    q_ref, c_ref, gq_ref, gc_ref, slope_ref, t_ref, tgt_ref,
    loss_ref, ug_ref, ig_ref, ugate_ref, igate_ref,
    qall, ugall, call, giall, gstage, gpad, git, qm, gub, tgtb,
    logit, weight, score, dinv, mx, ps, stat, ltb,
    lg, igp, ugv, uacc, ibuf, sbuf, rbuf, igsend, igrecv,
    urecv, ured, usend, uxrecv, ifin, irecv, igx, ugsend, ugrecv,
    x_s, x_r, q_s, q_r, u_s, u_r, gi_s, gi_r, ag_s, ag_r, st_s, st_r,
    rs_s, rs_r, ig_s, ig_r, fx_s, fx_r, ugs_s, ugs_r,
):
    blk = lax.axis_index("blk")
    x = lax.axis_index("comp")
    z = blk // 2
    c = lax.rem(blk, 2)
    me = 2 * x + c

    def dev(zz, cc, xx):
        return {"blk": lax.rem(zz + NZ, NZ) * 2 + cc, "comp": xx}

    def rc(src, dst, ss, rs, device):
        return pltpu.make_async_remote_copy(
            src_ref=src, dst_ref=dst, send_sem=ss, recv_sem=rs, device_id=device, device_id_type=MESH
        )

    xp, cp, dp = dev(z, c, 1 - x), dev(z, 1 - c, x), dev(z, 1 - c, 1 - x)
    quad = (xp, cp, dp)

    own_rows = pl.ds(pl.multiple_of(x * CH, CH), CH)
    peer_rows = pl.ds(pl.multiple_of((1 - x) * CH, CH), CH)
    call[z, x] = c_ref[own_rows, :]
    qall[c, x] = q_ref[...]
    gc = gc_ref[...].astype(F32)
    gc = jnp.concatenate([gc, gc], axis=0)
    low = jnp.broadcast_to(x, (8, CH)) == 0
    giall[z, x] = jnp.where(low, gc[:, :CH], gc[:, CH:])
    gstage[...] = jnp.where(low, gc[:, CH:], gc[:, :CH])
    gq = gq_ref[...].astype(F32)
    ugall[me] = jnp.concatenate([gq, jnp.broadcast_to(tgt_ref[...].astype(F32), (4, UB))], axis=0)

    barrier = pltpu.get_barrier_semaphore()
    for d in range(1, NZ):
        pl.semaphore_signal(barrier, inc=1, device_id=dev(z + d, c, x), device_id_type=MESH)
    for peer in quad:
        pl.semaphore_signal(barrier, inc=1, device_id=peer, device_id_type=MESH)
    pl.semaphore_wait(barrier, NZ - 1 + 3)

    def hop(dr, s, h):
        step = 1 - 2 * dr
        o = lax.rem(z - step * (s - 1) + NZ, NZ)
        return rc(
            call.at[o, h], call.at[o, h], ag_s.at[dr, s - 1, h], ag_r.at[dr, s - 1, h],
            dev(z + step, c, x),
        )

    x_item = rc(c_ref.at[peer_rows, :], call.at[z, x], x_s.at[0], x_r.at[0], xp)
    x_gate = rc(gstage, giall.at[z, x], x_s.at[1], x_r.at[1], xp)
    q_x = rc(q_ref, qall.at[c, x], q_s.at[0], q_r.at[0], xp)
    q_c = rc(q_ref, qall.at[c, x], q_s.at[1], q_r.at[1], cp)
    q_f = rc(qall.at[c, 1 - x], qall.at[c, 1 - x], q_s.at[2], q_r.at[2], cp)
    u_sends = [rc(ugall.at[me], ugall.at[me], u_s.at[i], u_r.at[i], quad[i]) for i in range(3)]
    x_item.start()
    x_gate.start()
    hop(0, 1, x).start()
    hop(1, 1, x).start()
    q_x.start()
    q_c.start()
    for s in u_sends:
        s.start()

    def gi_copy(d):
        return rc(giall.at[z], giall.at[z], gi_s.at[d], gi_r.at[d], dev(z + d, c, x))

    x_item.wait_recv()
    hop(0, 1, 1 - x).start()
    hop(1, 1, 1 - x).start()
    x_gate.wait_recv()

    def gi_start(d, carry):
        gi_copy(d).start()
        return carry

    lax.fori_loop(1, NZ, gi_start, 0)
    q_x.wait_recv()
    q_f.start()
    for s in u_sends:
        s.wait_recv()

    gpad[...] = jnp.zeros_like(gpad)
    mx[...] = jnp.full(mx.shape, -jnp.inf, F32)
    ps[...] = jnp.zeros_like(ps)
    uacc[...] = jnp.zeros_like(uacc)
    ugv[...] = jnp.zeros_like(ugv)
    for k in range(K):
        h, r = k // 4, k % 4
        row = jnp.concatenate([ugall[2 * h, r : r + 1, :], ugall[2 * h + 1, r : r + 1, :]], axis=1)
        gub[k] = jnp.broadcast_to(row * LOG2E, (8, US))
    tgtb[...] = jnp.broadcast_to(
        jnp.concatenate([ugall[0, 4:5, :], ugall[1, 4:5, :]], axis=1), (8, US)
    )
    q_c.wait_recv()
    q_f.wait_recv()
    lane = lax.broadcasted_iota(jnp.int32, (UB, CH), 1)
    for h in range(2):
        for p in range(2):
            for cc in range(2):
                pair = qall[cc, h, :, p * CH : (p + 1) * CH].astype(F32)
                k = 4 * h + 2 * p
                qm[k, cc * UB : (cc + 1) * UB, :] = jnp.where(lane < 64, pair, 0.0).astype(BF16)
                qm[k + 1, cc * UB : (cc + 1) * UB, :] = jnp.where(lane < 64, 0.0, pair).astype(BF16)

    inv_t = 1.0 / jnp.full((8, US), t_ref[0], F32)
    inv_t16 = jnp.concatenate([inv_t, inv_t], axis=0)
    row_iota = lax.broadcasted_iota(jnp.int32, (ROWS, US), 0)

    def twice(v):
        return jnp.concatenate([v, v], axis=0)

    def is_positive(o, r):
        ids = row_iota + ((o * 2 + c) * UB + x * CH + r * ROWS)
        return twice(tgtb[...]) == ids.astype(F32)

    def forward(j, carry):
        s = (j + 1) // 2
        odd = lax.rem(j, 2) == 1

        @pl.when(odd)
        def _():
            for dr in range(2):
                for h in range(2):
                    last = 4 if h == dr else 3

                    @pl.when(s <= last)
                    def _():
                        hop(dr, s, h).wait_recv()

                    @pl.when(s < last)
                    def _():
                        hop(dr, s + 1, h).start()

            gi_copy(s).wait_recv()

            @pl.when(s < 4)
            def _():
                gi_copy(NZ - s).wait_recv()

        o = lax.rem(z + NZ + jnp.where(odd, -s, s), NZ)
        gpad[0:8, :] = giall[o, 0]
        gpad[8:16, :] = giall[o, 1]
        git[...] = gpad[...].T * LOG2E
        for k in range(K):
            h, p = k // 4, (k % 4) // 2
            logit[o, k] = lax.dot_general(
                call[o, h, :, p * CH : (p + 1) * CH], qm[k], NT, preferred_element_type=F32
            )

        def rows_of(r, carry):
            top, pos = carry
            rows = pl.ds(pl.multiple_of(r * ROWS, ROWS), ROWS)
            den = num = None
            gcols = git[rows, :]
            for k in range(K):
                col = (k // 4) * 8 + k % 4
                l = logit[o, k, rows, :]
                e = jnp.tanh(l) * (slope_ref[k] * LOG2E) + gcols[:, col : col + 1] + twice(gub[k])
                w = jnp.exp2(e)
                weight[o, k, rows, :] = w
                wl = w * l
                den = w if den is None else den + w
                num = wl if num is None else num + wl
            di = 1.0 / den
            sc = num * di
            dinv[o, rows, :] = di
            score[o, rows, :] = sc
            hit = jnp.where(is_positive(o, r), sc, 0.0)
            return (
                jnp.maximum(top, jnp.maximum(sc[:8], sc[8:])),
                pos + hit[:8] + hit[8:],
            )

        top, pos = lax.fori_loop(0, CH // ROWS, rows_of, (mx[...], ps[...]))
        mx[...] = top
        ps[...] = pos
        return carry

    lax.fori_loop(0, NZ, forward, 0)

    top = jnp.max(mx[...], axis=0, keepdims=True)
    scale2 = inv_t * LOG2E
    shift = jnp.broadcast_to(top, (8, US)) * scale2

    def sum_exp(i, acc):
        o = i // 4
        rows = pl.ds(pl.multiple_of(lax.rem(i, 4) * 32, 32), 32)
        v = score[o, rows, :]
        for m in range(4):
            acc = acc + jnp.exp2(v[m * 8 : (m + 1) * 8] * scale2 - shift)
        return acc

    total = lax.fori_loop(0, NZ * 4, sum_exp, jnp.zeros((8, US), F32))
    stat[me, 0:1, :] = top
    stat[me, 1:2, :] = jnp.sum(total, axis=0, keepdims=True)
    stat[me, 2:3, :] = jnp.sum(ps[...], axis=0, keepdims=True)
    stat[me, 3:8, :] = jnp.zeros((5, US), F32)
    st_sends = [rc(stat.at[me], stat.at[me], st_s.at[i], st_r.at[i], quad[i]) for i in range(3)]
    for s in st_sends:
        s.start()
    for s in st_sends:
        s.wait_recv()
    st = [stat[i] for i in range(4)]
    all_top = jnp.maximum(jnp.maximum(st[0][0:1], st[1][0:1]), jnp.maximum(st[2][0:1], st[3][0:1]))
    inv_row = inv_t[0:1]
    all_sum = all_pos = None
    for i in range(4):
        part = st[i][1:2] * jnp.exp((st[i][0:1] - all_top) * inv_row)
        all_sum = part if all_sum is None else all_sum + part
        all_pos = st[i][2:3] if all_pos is None else all_pos + st[i][2:3]
    log_total = all_top * inv_row + jnp.log(all_sum)
    loss = log_total - all_pos * inv_row
    loss_ref[...] = jnp.where(jnp.broadcast_to(c, (1, UB)) == 0, loss[:, :UB], loss[:, UB:])
    ltb[...] = jnp.broadcast_to(log_total * LOG2E, (8, US))

    ones_row = lax.broadcasted_iota(jnp.int32, (K, K * CH), 0)
    ones_col = lax.broadcasted_iota(jnp.int32, (K, K * CH), 1) // CH
    ones = jnp.where(ones_row == ones_col, 1.0, 0.0).astype(BF16)

    def ig_copy(d):
        return rc(igsend.at[d], igrecv.at[d], ig_s.at[d], ig_r.at[d], dev(z + d, c, x))

    def rs_copy(dr, i, h):
        return rc(
            sbuf.at[dr, i, h], rbuf.at[dr, i, h], rs_s.at[dr, i, h], rs_r.at[dr, i, h],
            dev(z + 2 * dr - 1, c, x),
        )

    def backward(j, carry):
        d = 4 - (j + 1) // 2
        odd = lax.rem(j, 2) == 1
        o = lax.rem(z + NZ + jnp.where(odd, -d, d), NZ)

        def rows_of(r, carry):
            rows = pl.ds(pl.multiple_of(r * ROWS, ROWS), ROWS)
            sc = score[o, rows, :]
            soft = jnp.exp2(sc * twice(scale2) - twice(ltb[...]))
            soft = jnp.where(is_positive(o, r), soft - 1.0, soft) * inv_t16
            share = soft * dinv[o, rows, :]
            for k in range(K):
                l = logit[o, k, rows, :]
                t = jnp.tanh(l)
                g = weight[o, k, rows, :] * share
                gg = g * (l - sc)
                sk = slope_ref[k]
                out = g + gg * (sk - (t * t) * sk)
                lg[k, rows, :] = out.astype(BF16)
                ugv[k] = ugv[k] + (gg[:8] + gg[8:])
                igp[rows, k * CH : (k + 1) * CH] = (gg[:, 0:128] + gg[:, 128:256]) + (
                    gg[:, 256:384] + gg[:, 384:512]
                )
            return carry

        lax.fori_loop(0, CH // ROWS, rows_of, 0)
        for h in range(2):
            for p in range(2):
                k = 4 * h + 2 * p
                ibuf[h, :, p * CH : (p + 1) * CH] = jnp.dot(
                    lg[k], qm[k], preferred_element_type=F32
                ) + jnp.dot(lg[k + 1], qm[k + 1], preferred_element_type=F32)
        hi = igp[...].astype(BF16)
        lo = (igp[...] - hi.astype(F32)).astype(BF16)
        gate = lax.dot_general(ones, hi, NT, preferred_element_type=F32) + lax.dot_general(
            ones, lo, NT, preferred_element_type=F32
        )

        to = lax.rem(o - z + NZ, NZ)

        @pl.when(j < 7)
        def _():
            igsend[to] = gate
            ig_copy(to).start()

        @pl.when(j == 7)
        def _():
            igrecv[0] = gate

        @pl.when(j == 0)
        def _():
            for h in range(2):
                sbuf[h, 3, h] = ibuf[h].astype(BF16)
                rs_copy(h, 3, h).start()

        @pl.when((j > 0) & (j < 7))
        def _():
            dr = 1 - lax.rem(j, 2)
            for h in range(2):

                @pl.when((d < 3) | (dr == h))
                def _():
                    rs_copy(dr, d, h).wait_recv()
                    ibuf[h] = ibuf[h] + rbuf[dr, d, h].astype(F32)

                sbuf[dr, d - 1, h] = ibuf[h].astype(BF16)
                rs_copy(dr, d - 1, h).start()

        for h in range(2):
            for p in range(2):
                k = 4 * h + 2 * p
                ct = call[o, h, :, p * CH : (p + 1) * CH].T
                for kk in range(2):
                    part = jnp.dot(
                        ct[kk * 64 : (kk + 1) * 64], lg[k + kk], preferred_element_type=F32
                    )
                    at = slice((k + kk) * 64, (k + kk + 1) * 64)
                    uacc[0, at, :] += part[:, :UB]
                    uacc[1, at, :] += part[:, UB:]
        return carry

    lax.fori_loop(0, NZ, backward, 0)

    u_core = rc(uacc.at[1 - c], urecv, fx_s.at[0], fx_r.at[0], cp)
    u_core.start()
    for k in range(K):
        ugsend[k : k + 1, :] = jnp.sum(ugv[k], axis=0, keepdims=True)
    ug_sends = [rc(ugsend, ugrecv.at[i], ugs_s.at[i], ugs_r.at[i], quad[i]) for i in range(3)]
    for s in ug_sends:
        s.start()
    u_core.wait_recv()
    ured[...] = uacc[c] + urecv[...]
    half_other = pl.ds(pl.multiple_of((1 - x) * UB, UB), UB)
    half_own = pl.ds(pl.multiple_of(x * UB, UB), UB)
    usend[...] = ured[half_other, :].astype(BF16)
    u_x = rc(usend, uxrecv, fx_s.at[1], fx_r.at[1], xp)
    u_x.start()

    for dr in range(2):
        for h in range(2):
            rs_copy(dr, 0, h).wait_recv()
    for h in range(2):
        ifin[h] = ibuf[h] + (rbuf[0, 0, h].astype(F32) + rbuf[1, 0, h].astype(F32))
    i_x = rc(ifin.at[1 - x], irecv, fx_s.at[2], fx_r.at[2], xp)
    i_x.start()
    for d in range(1, NZ):
        ig_copy(d).wait_recv()
    gate = igrecv[0]
    for d in range(1, NZ):
        gate = gate + igrecv[d]
    igx[0] = gate
    ig_x = rc(igx.at[0], igx.at[1], fx_s.at[3], fx_r.at[3], xp)
    ig_x.start()
    ig_ref[own_rows, :] = ifin[x]

    for s in ug_sends:
        s.wait_recv()
    ugate = (ugsend[...] + ugrecv[0]) + (ugrecv[1] + ugrecv[2])
    ugate = jnp.where(jnp.broadcast_to(c, (K, UB)) == 0, ugate[:, :UB], ugate[:, UB:])
    ugate_ref[...] = jnp.where(jnp.broadcast_to(x, (4, UB)) == 0, ugate[:4], ugate[4:])

    ig_x.wait_recv()
    mine, theirs = igx[0], igx[1]
    upper = jnp.concatenate([mine, theirs], axis=1)[:4]
    lower = jnp.concatenate([theirs, mine], axis=1)[4:]
    igate_ref[...] = jnp.where(jnp.broadcast_to(x, (4, UB)) == 0, upper, lower)

    u_x.wait_recv()
    ug_ref[...] = (ured[half_own, :] + uxrecv[...].astype(F32)).T
    i_x.wait_recv()
    ig_ref[peer_rows, :] = irecv[...]

    for s in (x_item, x_gate, q_x, q_c, q_f, *u_sends, *st_sends, u_core, u_x, i_x, ig_x, *ug_sends):
        s.wait_send()
    for d in range(1, NZ):
        gi_copy(d).wait_send()
        ig_copy(d).wait_send()
    for dr in range(2):
        for h in range(2):
            for s in range(1, 5 if h == dr else 4):
                hop(dr, s, h).wait_send()
                rs_copy(dr, s - 1, h).wait_send()


def body(query, candidate, query_gate, candidate_gate, slope, scale, target):
    vmem = pl.BlockSpec(memory_space=pltpu.VMEM)
    smem = pl.BlockSpec(memory_space=pltpu.SMEM)
    dma = pltpu.SemaphoreType.DMA
    scratch = [
        pltpu.VMEM((2, 2, UB, UB), BF16),
        pltpu.VMEM((4, 8, UB), F32),
        pltpu.VMEM((NZ, 2, CH, UB), BF16),
        pltpu.VMEM((NZ, 2, 8, CH), F32),
        pltpu.VMEM((8, CH), F32),
        pltpu.VMEM((CH, CH), F32),
        pltpu.VMEM((CH, CH), F32),
        pltpu.VMEM((K, US, CH), BF16),
        pltpu.VMEM((K, 8, US), F32),
        pltpu.VMEM((8, US), F32),
        pltpu.VMEM((NZ, K, CH, US), F32),
        pltpu.VMEM((NZ, K, CH, US), F32),
        pltpu.VMEM((NZ, CH, US), F32),
        pltpu.VMEM((NZ, CH, US), F32),
        pltpu.VMEM((8, US), F32),
        pltpu.VMEM((8, US), F32),
        pltpu.VMEM((4, 8, US), F32),
        pltpu.VMEM((8, US), F32),
        pltpu.VMEM((K, CH, US), BF16),
        pltpu.VMEM((CH, K * CH), F32),
        pltpu.VMEM((K, 8, US), F32),
        pltpu.VMEM((2, US, UB), F32),
        pltpu.VMEM((2, CH, UB), F32),
        pltpu.VMEM((2, 4, 2, CH, UB), BF16),
        pltpu.VMEM((2, 4, 2, CH, UB), BF16),
        pltpu.VMEM((NZ, K, CH), F32),
        pltpu.VMEM((NZ, K, CH), F32),
        pltpu.VMEM((US, UB), F32),
        pltpu.VMEM((US, UB), F32),
        pltpu.VMEM((UB, UB), BF16),
        pltpu.VMEM((UB, UB), BF16),
        pltpu.VMEM((2, CH, UB), F32),
        pltpu.VMEM((CH, UB), F32),
        pltpu.VMEM((2, K, CH), F32),
        pltpu.VMEM((K, US), F32),
        pltpu.VMEM((3, K, US), F32),
        dma((2,)), dma((2,)),
        dma((3,)), dma((3,)),
        dma((3,)), dma((3,)),
        dma((NZ,)), dma((NZ,)),
        dma((2, 4, 2)), dma((2, 4, 2)),
        dma((3,)), dma((3,)),
        dma((2, 4, 2)), dma((2, 4, 2)),
        dma((NZ,)), dma((NZ,)),
        dma((4,)), dma((4,)),
        dma((3,)), dma((3,)),
    ]
    loss, ug, ig, ugate, igate = pl.pallas_call(
        kernel,
        out_shape=(
            jax.ShapeDtypeStruct((1, UB), F32),
            jax.ShapeDtypeStruct((UB, UB), F32),
            jax.ShapeDtypeStruct((UB, UB), F32),
            jax.ShapeDtypeStruct((4, UB), F32),
            jax.ShapeDtypeStruct((4, UB), F32),
        ),
        in_specs=[vmem, vmem, vmem, vmem, smem, smem, vmem],
        out_specs=(vmem,) * 5,
        scratch_shapes=scratch,
        compiler_params=pltpu.CompilerParams(
            collective_id=0, has_side_effects=True, vmem_limit_bytes=60 * 1024 * 1024
        ),
    )(query, candidate, query_gate, candidate_gate, slope, scale, target.reshape(1, UB))
    return loss.reshape(UB), ug, ig, ugate, igate


def solution(mesh):
    in_specs = (
        P(("task", "blk"), "comp"),
        P(("task", "blk"), "comp"),
        P("comp", ("task", "blk")),
        P("comp", ("task", "blk")),
        P(),
        P("task"),
        P(("task", "blk")),
    )
    out_specs = (
        P(("task", "blk")),
        P(("task", "blk"), "comp"),
        P(("task", "blk"), "comp"),
        P("comp", ("task", "blk")),
        P("comp", ("task", "blk")),
    )
    return jax.shard_map(body, mesh=mesh, in_specs=in_specs, out_specs=out_specs, check_vma=False)
```

time: 979 us -> 72.7 us (0.07)
  waiting for transfers between devices: 721 us -> 0 us
  starting transfers between devices: 96.1 us -> 0 us
  other arithmetic: 84.6 us -> 0 us
  Pallas kernels: 0 us -> 66.3 us
  matrix products: 42.1 us -> 0 us
  between operations: 16 us -> 1.3 us
    psum x16 -> x0, waiting for transfers between devices: 679 us -> none  [forward_step(): denominator, numerator = lax.psum((denom_part, numer_part), 'comp')]
    ppermute x92 -> x0, starting transfers between devices: 95.4 us -> none  [passed_along(): return lax.ppermute(block, axis, route)]
    pallas_call x0 -> x1, Pallas kernels: none -> 66.3 us  [body(): pl.pallas_call(kernel, out_shape=(jax.ShapeDtypeStruct((1, UB), F32), jax...]
    dot_general x64 -> x0, matrix products: 42.1 us -> none  [the longest x32 34.1 us: pair_terms(): jnp.einsum('rke,ike->kri', user_split, item_split, preferred_element_type...]
    ppermute x92 -> x0, waiting for transfers between devices: 41.8 us -> none  [passed_along(): return lax.ppermute(block, axis, route)]
    dynamic_update_slice x15 -> x0, other arithmetic: 27.8 us -> none  [forward_step(): denoms = lax.dynamic_update_index_in_dim(denoms, denominator, step_index, 0)]
    mul x15 -> x0, other arithmetic: 27.2 us -> none  [back_step(): softmax_grad[None] * gate_share]
    reduce_sum x33 -> x0, other arithmetic: 23.6 us -> none  [the longest x16 19.2 us: forward_step(): pos_score = pos_score + jnp.sum(positives(step_index) * pair_score, axis=1)]
  transfers between devices with their start and end apart: 108 -> 0, of which waited for: 32 -> 0; matrix products, arithmetic and copies ran while one was open for 10% -> 0% of each run, Pallas kernels for 0% -> 0%
where the time goes in v1:
time: 72.7 us; the launch traced here: 72.5 us
  Pallas kernels  66.3 us (91%)
  local copies, waits for them, and re-layouts  4.91 us (7%)
  between operations  1.3 us (2%)
    pallas_call x1, Pallas kernels, body(): pl.pallas_call(kernel, out_shape=(jax.ShapeDtypeStruct((1, UB), F32), jax...  66.3 us
    unnamed x13, local copies, waits for them, and re-layouts  4.91 us

profile of v1, /device:TPU:1, one launch (start us, length us, event | category | flops | bytes accessed | tf_op | source)
XLA Modules:
  0.0 72.5 jit_solution(7887560053295154326)
XLA Ops:
  1.3 66.3 %shard_map.110 = (f32[1,256]{1,0:T(1,128)}, f32[256,256]{1,0:T(8,128)}, f32[256,256]{1,0:T(8,128)}, f32[4,256]{1,0:T(4,128)}, f32[4,256]{1,0:T(4,128)}) custom-call(bf16[256,256]{1,0:T(8,128)(2,1)} %q_ref.1, bf16[256,256]{1,0:T(8,128)(2,1)} %c_ref.1, bf16[4,256]{1,0:T(4,128)(2,1)} %gq_ref.1, bf16[4,256]{1,0:T(4,128)(2,1)} %gc_ref.1, f32[8]{0:T(128)} %slope_ref.1, ...), custom_call_target="tpu_custom_call" | custom-call | tf_op jit(solution)/shard_map/pallas_call | solution.py:450
  67.5 0.0 copy-start.3
  67.5 0.7 copy-done.3
  68.2 0.6 copy.18
  68.8 0.0 copy-start
  68.8 1.7 %copy.19 = f32[256,256]{1,0:T(8,128)} copy(f32[256,256]{1,0:T(8,128)} %get-tuple-element.21) | data formatting | bytes 524288
  70.5 0.0 copy-done
  70.5 0.0 copy-start.2
  70.5 0.7 copy.20
  71.2 0.0 copy-done.2
  71.2 0.0 copy-start.1
  71.2 0.6 copy.21
  71.8 0.1 copy-done.1
  71.9 0.6 copy.22
Async XLA Ops:
  67.5 0.7 copy-start.3
  68.8 1.7 %copy-start = (f32[256,256]{1,0:T(8,128)S(1)}, f32[256,256]{1,0:T(8,128)}, u32[]{:S(2)}) copy-start(f32[256,256]{1,0:T(8,128)} %get-tuple-element.22) | copy-start | bytes 786436
  70.5 0.7 copy-start.2
  71.2 0.7 copy-start.1

commit v2 on v1

v2 whole, which is shorter than its diff:
```python
import jax
import jax.numpy as jnp
from jax import lax
from jax.experimental import pallas as pl
from jax.experimental.pallas import tpu as pltpu
from jax.sharding import PartitionSpec as P

MESH = pl.DeviceIdType.MESH
LOG2E = 1.4426950408889634
F32, BF16 = jnp.float32, jnp.bfloat16
NZ = 8
UB = 256
US = 512
CH = 128
SLOT = CH + 16
PIECES = ((0, 80), (80, 64))
K = 8
ROWS = 16
NT = (((1,), (1,)), ((), ()))


def kernel(
    q_ref, c_ref, gq_ref, gc_ref, slope_ref, t_ref, tgt_ref,
    loss_ref, ug_ref, ig_ref, ugate_ref, igate_ref,
    qall, ugall, call, xstage, gpad, git, ctall, qm, gub, tgtb,
    logit, weight, score, dinv, mx, sm, ps, stat, ltb,
    lg, igp, ugv, uacc, ibk, sbuf, rbuf, gsend, grecv,
    urecv, ukeep, usend, uxrecv, isend, irecv, igx, ugsend, ugrecv,
    x_s, x_r, q_s, q_r, u_s, u_r, ag_s, ag_r, st_s, st_r,
    rs_s, rs_r, g_s, g_r, uc_s, uc_r, ux_s, ux_r, fx_s, fx_r, ugs_s, ugs_r,
):
    blk = lax.axis_index("blk")
    x = lax.axis_index("comp")
    z = blk // 2
    c = lax.rem(blk, 2)
    me = 2 * x + c

    def dev(zz, cc, xx):
        return {"blk": lax.rem(zz + NZ, NZ) * 2 + cc, "comp": xx}

    def rc(src, dst, ss, rs, device):
        return pltpu.make_async_remote_copy(
            src_ref=src, dst_ref=dst, send_sem=ss, recv_sem=rs, device_id=device, device_id_type=MESH
        )

    xp, cp, dp = dev(z, c, 1 - x), dev(z, 1 - c, x), dev(z, 1 - c, 1 - x)
    quad = (xp, cp, dp)

    barrier = pltpu.get_barrier_semaphore()
    near = [dev(z + d, c, x) for d in (-2, -1, 1, 2)] + [dev(z + d, c, 1 - x) for d in (-1, 1)]
    for peer in (*quad, *near):
        pl.semaphore_signal(barrier, inc=1, device_id=peer, device_id_type=MESH)

    own_rows = pl.ds(pl.multiple_of(x * CH, CH), CH)
    peer_rows = pl.ds(pl.multiple_of((1 - x) * CH, CH), CH)
    gc = gc_ref[...].astype(F32)
    gc = jnp.concatenate([gc, gc], axis=0)
    gc = jnp.concatenate([gc, gc], axis=0)
    low = jnp.broadcast_to(x, (16, CH)) == 0
    blank = jnp.zeros((16, CH), F32)
    own_gate = jnp.concatenate([jnp.where(low, gc[:, :CH], gc[:, CH:]), blank], axis=1)
    peer_gate = jnp.concatenate([jnp.where(low, gc[:, CH:], gc[:, :CH]), blank], axis=1)
    call[z, x, :CH, :] = c_ref[own_rows, :]
    call[z, x, CH:, :] = own_gate.astype(BF16)
    xstage[:CH, :] = c_ref[peer_rows, :]
    xstage[CH:, :] = peer_gate.astype(BF16)
    qall[c, x] = q_ref[...]
    gq = gq_ref[...].astype(F32)
    ugall[me] = jnp.concatenate([gq, jnp.broadcast_to(tgt_ref[...].astype(F32), (4, UB))], axis=0)

    pl.semaphore_wait(barrier, len(quad) + len(near))

    def hop(dr, s, hh, n):
        step = 1 - 2 * dr
        o = lax.rem(z - step * (s - 1) + NZ, NZ)
        h = x if hh == 0 else 1 - x
        at = call.at[o, h, pl.ds(*PIECES[n]), :]
        return rc(at, at, ag_s.at[dr, s - 1, hh, n], ag_r.at[dr, s - 1, hh, n], dev(z + step, c, x))

    x_item = rc(xstage, call.at[z, x], x_s.at[0], x_r.at[0], xp)
    q_x = rc(q_ref, qall.at[c, x], q_s.at[0], q_r.at[0], xp)
    q_c = rc(q_ref, qall.at[c, x], q_s.at[1], q_r.at[1], cp)
    q_f = rc(qall.at[c, 1 - x], qall.at[c, 1 - x], q_s.at[2], q_r.at[2], cp)
    u_sends = [rc(ugall.at[me], ugall.at[me], u_s.at[i], u_r.at[i], quad[i]) for i in range(3)]
    x_item.start()
    for n in range(2):
        hop(0, 1, 0, n).start()
        hop(1, 1, 0, n).start()
    q_x.start()
    for s in u_sends:
        s.start()
    q_c.start()

    gpad[...] = jnp.zeros_like(gpad)
    mx[...] = jnp.full(mx.shape, -3.0e38, F32)
    sm[...] = jnp.zeros_like(sm)
    ps[...] = jnp.zeros_like(ps)
    uacc[...] = jnp.zeros_like(uacc)
    ugv[...] = jnp.zeros_like(ugv)
    lg[1] = jnp.zeros((K, CH, US), BF16)

    x_item.wait_recv()
    for n in range(2):
        hop(0, 1, 1, n).start()
        hop(1, 1, 1, n).start()
    q_x.wait_recv()
    q_f.start()

    lane = lax.broadcasted_iota(jnp.int32, (UB, CH), 1)

    def mask_users(cc, h):
        for p in range(2):
            pair = qall[cc, h, :, p * CH : (p + 1) * CH].astype(F32)
            k = 4 * h + 2 * p
            rows = pl.ds(pl.multiple_of(cc * UB, UB), UB)
            qm[k, rows, :] = jnp.where(lane < 64, pair, 0.0).astype(BF16)
            qm[k + 1, rows, :] = jnp.where(lane < 64, 0.0, pair).astype(BF16)

    for h in range(2):
        mask_users(c, h)
    for s in u_sends:
        s.wait_recv()
    for k in range(K):
        h, r = k // 4, k % 4
        row = jnp.concatenate([ugall[2 * h, r : r + 1, :], ugall[2 * h + 1, r : r + 1, :]], axis=1)
        gub[k] = jnp.broadcast_to(row * LOG2E, (8, US))
    tgtb[...] = jnp.broadcast_to(
        jnp.concatenate([ugall[0, 4:5, :], ugall[1, 4:5, :]], axis=1), (8, US)
    )
    q_c.wait_recv()
    q_f.wait_recv()
    for h in range(2):
        mask_users(1 - c, h)

    inv_t = 1.0 / jnp.full((8, US), t_ref[0], F32)
    inv_t16 = jnp.concatenate([inv_t, inv_t], axis=0)
    scale2 = inv_t * LOG2E
    row_iota = lax.broadcasted_iota(jnp.int32, (ROWS, US), 0)

    def twice(v):
        return jnp.concatenate([v, v], axis=0)

    def is_positive(o, r):
        ids = row_iota + ((o * 2 + c) * UB + x * CH + r * ROWS)
        return twice(tgtb[...]) == ids.astype(F32)

    def forward(j, carry):
        s = (j + 1) // 2
        odd = lax.rem(j, 2) == 1

        @pl.when(odd)
        def _():
            for hh in range(2):
                for n in range(2):
                    for dr in range(2):
                        last = 4 if hh == dr else 3

                        @pl.when(s <= last)
                        def _():
                            hop(dr, s, hh, n).wait_recv()

                        @pl.when(s < last)
                        def _():
                            hop(dr, s + 1, hh, n).start()

        o = lax.rem(z + NZ + jnp.where(odd, -s, s), NZ)
        gpad[0:16, :] = call[o, 0, CH:, :CH].astype(F32)
        gpad[16:32, :] = call[o, 1, CH:, :CH].astype(F32)
        git[...] = gpad[...].T * LOG2E
        for k in range(K):
            h, p = k // 4, (k % 4) // 2
            logit[o, k] = lax.dot_general(
                call[o, h, :CH, p * CH : (p + 1) * CH], qm[k], NT, preferred_element_type=F32
            )
        for h in range(2):
            for p in range(2):
                at = slice((2 * h + p) * CH, (2 * h + p + 1) * CH)
                ctall[o, at, :] = call[o, h, :CH, p * CH : (p + 1) * CH].T

        def rows_of(r, carry):
            top, pos = carry
            rows = pl.ds(pl.multiple_of(r * ROWS, ROWS), ROWS)
            den = num = None
            gcols = git[rows, :]
            for k in range(K):
                col = (k // 4) * 16 + k % 4
                l = logit[o, k, rows, :]
                e = jnp.tanh(l) * (slope_ref[k] * LOG2E) + gcols[:, col : col + 1] + twice(gub[k])
                w = jnp.exp2(e)
                weight[o, k, rows, :] = w
                wl = w * l
                den = w if den is None else den + w
                num = wl if num is None else num + wl
            di = 1.0 / den
            sc = num * di
            dinv[o, rows, :] = di
            score[o, rows, :] = sc
            hit = jnp.where(is_positive(o, r), sc, 0.0)
            return (
                jnp.maximum(top, jnp.maximum(sc[:8], sc[8:])),
                pos + hit[:8] + hit[8:],
            )

        before = mx[...]
        top, pos = lax.fori_loop(0, CH // ROWS, rows_of, (before, ps[...]))
        mx[...] = top
        ps[...] = pos
        shift = top * scale2
        total = sm[...] * jnp.exp2((before - top) * scale2)
        for m in range(CH // 8):
            total = total + jnp.exp2(score[o, m * 8 : (m + 1) * 8, :] * scale2 - shift)
        sm[...] = total
        return carry

    lax.fori_loop(0, NZ, forward, 0)

    top = jnp.max(mx[...], axis=0, keepdims=True)
    total = sm[...] * jnp.exp2((mx[...] - top) * scale2)
    stat[me] = jnp.concatenate(
        [
            top,
            jnp.sum(total, axis=0, keepdims=True),
            jnp.sum(ps[...], axis=0, keepdims=True),
            jnp.zeros((5, US), F32),
        ],
        axis=0,
    )
    st_sends = [rc(stat.at[me], stat.at[me], st_s.at[i], st_r.at[i], quad[i]) for i in range(3)]
    for s in st_sends:
        s.start()
    for s in st_sends:
        s.wait_recv()
    st = [stat[i] for i in range(4)]
    all_top = jnp.maximum(jnp.maximum(st[0][0:1], st[1][0:1]), jnp.maximum(st[2][0:1], st[3][0:1]))
    inv_row = inv_t[0:1]
    all_sum = all_pos = None
    for i in range(4):
        part = st[i][1:2] * jnp.exp((st[i][0:1] - all_top) * inv_row)
        all_sum = part if all_sum is None else all_sum + part
        all_pos = st[i][2:3] if all_pos is None else all_pos + st[i][2:3]
    log_total = all_top * inv_row + jnp.log(all_sum)
    loss = log_total - all_pos * inv_row
    loss_ref[...] = jnp.where(jnp.broadcast_to(c, (1, UB)) == 0, loss[:, :UB], loss[:, UB:])
    ltb[...] = jnp.broadcast_to(log_total * LOG2E, (8, US))

    ones_row = lax.broadcasted_iota(jnp.int32, (K, K * CH), 0)
    ones_col = lax.broadcasted_iota(jnp.int32, (K, K * CH), 1) // CH
    ones = jnp.where(ones_row == ones_col, 1.0, 0.0).astype(BF16)

    def gate_copy(dr, d):
        far = 2 if d in (2, 4) else 1
        return rc(
            gsend.at[dr, d - 1], grecv.at[dr, d - 1], g_s.at[dr, d - 1], g_r.at[dr, d - 1],
            dev(z + far * (2 * dr - 1), c, x),
        )

    def rs_copy(dr, d, h):
        far = 2 if d in (2, 4) else 1
        return rc(
            sbuf.at[dr, d - 1, h], rbuf.at[dr, d - 1, h], rs_s.at[dr, d - 1, h], rs_r.at[dr, d - 1, h],
            dev(z + far * (2 * dr - 1), c, x),
        )

    def last_copy(dr, w):
        h = x if w == 0 else 1 - x
        return rc(
            sbuf.at[dr, 0, h], rbuf.at[dr, 0, w], rs_s.at[dr, 0, w], rs_r.at[dr, 0, w],
            dev(z + 2 * dr - 1, c, h),
        )

    def far_of(j):
        d = 4 - (j + 1) // 2
        return d, lax.rem(z + NZ + jnp.where(lax.rem(j, 2) == 1, -d, d), NZ)

    def matmuls(o, b, k):
        ibk[k] = jnp.dot(lg[b, k], qm[k], preferred_element_type=F32)
        at = pl.ds(pl.multiple_of(k * 64, 64), 64)
        part = jnp.dot(ctall[o, at, :], lg[b, k], preferred_element_type=F32)
        uacc[0, at, :] += part[:, :UB]
        uacc[1, at, :] += part[:, UB:]

    def item_sum(h):
        return jnp.concatenate([ibk[4 * h] + ibk[4 * h + 1], ibk[4 * h + 2] + ibk[4 * h + 3]], axis=1)

    def backward(j, carry):
        d, o = far_of(j)
        before = jnp.maximum(j - 1, 0)
        d_before, o_before = far_of(before)
        b = lax.rem(j, 2)

        def rows_of(r, carry):
            rows = pl.ds(pl.multiple_of(r * ROWS, ROWS), ROWS)
            matmuls(o_before, 1 - b, r)
            sc = score[o, rows, :]
            soft = jnp.exp2(sc * twice(scale2) - twice(ltb[...]))
            soft = jnp.where(is_positive(o, r), soft - 1.0, soft) * inv_t16
            share = soft * dinv[o, rows, :]
            for k in range(K):
                l = logit[o, k, rows, :]
                t = jnp.tanh(l)
                g = weight[o, k, rows, :] * share
                gg = g * (l - sc)
                sk = slope_ref[k]
                out = g + gg * (sk - (t * t) * sk)
                lg[b, k, rows, :] = out.astype(BF16)
                ugv[k] = ugv[k] + (gg[:8] + gg[8:])
                igp[rows, k * CH : (k + 1) * CH] = (gg[:, 0:128] + gg[:, 128:256]) + (
                    gg[:, 256:384] + gg[:, 384:512]
                )
            return carry

        lax.fori_loop(0, CH // ROWS, rows_of, 0)

        dr_before = 1 - lax.rem(before, 2)

        @pl.when(j == 1)
        def _():
            for h in range(2):
                sbuf[h, 3, h] = item_sum(h).astype(BF16)
                rs_copy(h, 4, h).start()

        for dr in range(2):
            mine = (j > 1) & (dr_before == dr)

            @pl.when(mine & (d_before == 3))
            def _():
                for h in range(2):
                    sbuf[dr, 2, h] = item_sum(h).astype(BF16)
                    rs_copy(dr, 3, h).start()

            @pl.when(mine & (d_before == 2))
            def _():
                for h in range(2):
                    rs_copy(dr, 3, h).wait_recv()
                    value = item_sum(h) + rbuf[dr, 2, h].astype(F32)
                    if h == dr:
                        rs_copy(dr, 4, h).wait_recv()
                        value = value + rbuf[dr, 3, h].astype(F32)
                    sbuf[dr, 1, h] = value.astype(BF16)
                    rs_copy(dr, 2, h).start()

            @pl.when(mine & (d_before == 1))
            def _():
                for h in range(2):
                    sbuf[dr, 0, h] = item_sum(h).astype(BF16)
                for w in (1, 0):
                    last_copy(dr, w).start()

        hi = igp[...].astype(BF16)
        lo = (igp[...] - hi.astype(F32)).astype(BF16)
        gate = lax.dot_general(ones, hi, NT, preferred_element_type=F32) + lax.dot_general(
            ones, lo, NT, preferred_element_type=F32
        )

        @pl.when(j == 0)
        def _():
            gsend[0, 3] = gate
            gate_copy(0, 4).start()

        @pl.when(j == 7)
        def _():
            igx[0] = gate

        for dr in range(2):
            mine = (j > 0) & (j < 7) & (lax.rem(j, 2) == 1 - dr)
            for dd in (1, 3):

                @pl.when(mine & (d == dd))
                def _():
                    gsend[dr, dd - 1] = gate
                    gate_copy(dr, dd).start()

            @pl.when(mine & (d == 2))
            def _():
                gate_copy(dr, 3).wait_recv()
                value = gate + grecv[dr, 2]
                if dr == 0:
                    gate_copy(0, 4).wait_recv()
                    value = value + grecv[0, 3]
                gsend[dr, 1] = value
                gate_copy(dr, 2).start()

        return carry

    lax.fori_loop(0, NZ, backward, 0)

    for k in range(K):
        ugsend[k : k + 1, :] = jnp.sum(ugv[k], axis=0, keepdims=True)
    ug_sends = [rc(ugsend, ugrecv.at[i], ugs_s.at[i], ugs_r.at[i], quad[i]) for i in range(3)]
    for s in ug_sends:
        s.start()

    def u_core(hh, p):
        h = 1 - x if hh == 0 else x
        at = pl.ds(pl.multiple_of(h * UB + p * CH, CH), CH)
        return rc(uacc.at[1 - c, at, :], urecv.at[hh, p], uc_s.at[hh, p], uc_r.at[hh, p], cp)

    def u_x(p):
        return rc(usend.at[p], uxrecv.at[p], ux_s.at[p], ux_r.at[p], xp)

    def core_sum(hh, p):
        h = 1 - x if hh == 0 else x
        at = pl.ds(pl.multiple_of(h * UB + p * CH, CH), CH)
        u_core(hh, p).wait_recv()
        return uacc[c, at, :] + urecv[hh, p]

    for hh in range(2):
        for p in range(2):
            for kk in range(2):
                h = 1 - x if hh == 0 else x
                matmuls(z, 1, 4 * h + 2 * p + kk)
            u_core(hh, p).start()
    for p in range(2):
        usend[p] = core_sum(0, p).astype(BF16)
        u_x(p).start()

    def own_sum(h):
        for dr in range(2):
            rs_copy(dr, 2, h).wait_recv()
        return item_sum(h) + (rbuf[0, 1, h].astype(F32) + rbuf[1, 1, h].astype(F32))

    sums = [own_sum(h) for h in range(2)]
    first = jnp.broadcast_to(x, (CH, UB)) == 0
    isend[...] = jnp.where(first, sums[1], sums[0]).astype(BF16)
    keep = jnp.where(first, sums[0], sums[1])
    i_x = rc(isend, irecv, fx_s.at[0], fx_r.at[0], xp)
    i_x.start()
    gate = igx[0]
    for dr in range(2):
        for d in (2, 1):
            gate_copy(dr, d).wait_recv()
            gate = gate + grecv[dr, d - 1]
    igx[0] = gate
    ig_x = rc(igx.at[0], igx.at[1], fx_s.at[1], fx_r.at[1], xp)
    ig_x.start()

    for p in range(2):
        ukeep[p * CH : (p + 1) * CH, :] = core_sum(1, p)
    for s in ug_sends:
        s.wait_recv()
    ugate = (ugsend[...] + ugrecv[0]) + (ugrecv[1] + ugrecv[2])
    ugate = jnp.where(jnp.broadcast_to(c, (K, UB)) == 0, ugate[:, :UB], ugate[:, UB:])
    ugate_ref[...] = jnp.where(jnp.broadcast_to(x, (4, UB)) == 0, ugate[:4], ugate[4:])

    for dr in range(2):
        last_copy(dr, 0).wait_recv()
    ig_ref[own_rows, :] = keep + (rbuf[0, 0, 0].astype(F32) + rbuf[1, 0, 0].astype(F32))
    for dr in range(2):
        last_copy(dr, 1).wait_recv()
    i_x.wait_recv()
    ig_ref[peer_rows, :] = irecv[...].astype(F32) + (
        rbuf[0, 0, 1].astype(F32) + rbuf[1, 0, 1].astype(F32)
    )
    ig_x.wait_recv()
    mine, theirs = igx[0], igx[1]
    upper = jnp.concatenate([mine, theirs], axis=1)[:4]
    lower = jnp.concatenate([theirs, mine], axis=1)[4:]
    igate_ref[...] = jnp.where(jnp.broadcast_to(x, (4, UB)) == 0, upper, lower)
    for p in range(2):
        u_x(p).wait_recv()
        at = slice(p * CH, (p + 1) * CH)
        ug_ref[:, at] = (ukeep[at, :] + uxrecv[p].astype(F32)).T

    for s in (x_item, q_x, q_c, q_f, *u_sends, *st_sends, i_x, ig_x, *ug_sends):
        s.wait_send()
    for p in range(2):
        u_x(p).wait_send()
        for hh in range(2):
            u_core(hh, p).wait_send()
    gate_copy(0, 4).wait_send()
    for dr in range(2):
        rs_copy(dr, 4, dr).wait_send()
        for d in (1, 2, 3):
            gate_copy(dr, d).wait_send()
        for w in range(2):
            last_copy(dr, w).wait_send()
            for d in (2, 3):
                rs_copy(dr, d, w).wait_send()
        for hh in range(2):
            for s in range(1, 5 if hh == dr else 4):
                for n in range(2):
                    hop(dr, s, hh, n).wait_send()


def write_out(loss, ug, ig, ugate, igate, *outs):
    for a, o in zip((loss, ug, ig, ugate, igate), outs):
        o[...] = a[...]


def body(query, candidate, query_gate, candidate_gate, slope, scale, target):
    vmem = pl.BlockSpec(memory_space=pltpu.VMEM)
    smem = pl.BlockSpec(memory_space=pltpu.SMEM)
    dma = pltpu.SemaphoreType.DMA
    scratch = [
        pltpu.VMEM((2, 2, UB, UB), BF16),
        pltpu.VMEM((4, 8, UB), F32),
        pltpu.VMEM((NZ, 2, SLOT, UB), BF16),
        pltpu.VMEM((SLOT, UB), BF16),
        pltpu.VMEM((CH, CH), F32),
        pltpu.VMEM((CH, CH), F32),
        pltpu.VMEM((NZ, K * 64, CH), BF16),
        pltpu.VMEM((K, US, CH), BF16),
        pltpu.VMEM((K, 8, US), F32),
        pltpu.VMEM((8, US), F32),
        pltpu.VMEM((NZ, K, CH, US), F32),
        pltpu.VMEM((NZ, K, CH, US), F32),
        pltpu.VMEM((NZ, CH, US), F32),
        pltpu.VMEM((NZ, CH, US), F32),
        pltpu.VMEM((8, US), F32),
        pltpu.VMEM((8, US), F32),
        pltpu.VMEM((8, US), F32),
        pltpu.VMEM((4, 8, US), F32),
        pltpu.VMEM((8, US), F32),
        pltpu.VMEM((2, K, CH, US), BF16),
        pltpu.VMEM((CH, K * CH), F32),
        pltpu.VMEM((K, 8, US), F32),
        pltpu.VMEM((2, US, UB), F32),
        pltpu.VMEM((K, CH, CH), F32),
        pltpu.VMEM((2, 4, 2, CH, UB), BF16),
        pltpu.VMEM((2, 4, 2, CH, UB), BF16),
        pltpu.VMEM((2, 4, K, CH), F32),
        pltpu.VMEM((2, 4, K, CH), F32),
        pltpu.VMEM((2, 2, CH, UB), F32),
        pltpu.VMEM((UB, UB), F32),
        pltpu.VMEM((2, CH, UB), BF16),
        pltpu.VMEM((2, CH, UB), BF16),
        pltpu.VMEM((CH, UB), BF16),
        pltpu.VMEM((CH, UB), BF16),
        pltpu.VMEM((2, K, CH), F32),
        pltpu.VMEM((K, US), F32),
        pltpu.VMEM((3, K, US), F32),
        dma((1,)), dma((1,)),
        dma((3,)), dma((3,)),
        dma((3,)), dma((3,)),
        dma((2, 4, 2, 2)), dma((2, 4, 2, 2)),
        dma((3,)), dma((3,)),
        dma((2, 4, 2)), dma((2, 4, 2)),
        dma((2, 4)), dma((2, 4)),
        dma((2, 2)), dma((2, 2)),
        dma((2,)), dma((2,)),
        dma((2,)), dma((2,)),
        dma((3,)), dma((3,)),
    ]
    outs = (
        jax.ShapeDtypeStruct((1, UB), F32),
        jax.ShapeDtypeStruct((UB, UB), F32),
        jax.ShapeDtypeStruct((UB, UB), F32),
        jax.ShapeDtypeStruct((4, UB), F32),
        jax.ShapeDtypeStruct((4, UB), F32),
    )
    results = pl.pallas_call(
        kernel,
        out_shape=outs,
        in_specs=[vmem, vmem, vmem, vmem, smem, smem, vmem],
        out_specs=(vmem,) * 5,
        scratch_shapes=scratch,
        compiler_params=pltpu.CompilerParams(
            collective_id=0, has_side_effects=True, vmem_limit_bytes=60 * 1024 * 1024
        ),
    )(query, candidate, query_gate, candidate_gate, slope, scale, target.reshape(1, UB))
    loss, ug, ig, ugate, igate = pl.pallas_call(
        write_out, out_shape=outs, in_specs=[vmem] * 5, out_specs=(vmem,) * 5
    )(*results)
    return loss.reshape(UB), ug, ig, ugate, igate


def solution(mesh):
    in_specs = (
        P(("task", "blk"), "comp"),
        P(("task", "blk"), "comp"),
        P("comp", ("task", "blk")),
        P("comp", ("task", "blk")),
        P(),
        P("task"),
        P(("task", "blk")),
    )
    out_specs = (
        P(("task", "blk")),
        P(("task", "blk"), "comp"),
        P(("task", "blk"), "comp"),
        P("comp", ("task", "blk")),
        P("comp", ("task", "blk")),
    )
    return jax.shard_map(body, mesh=mesh, in_specs=in_specs, out_specs=out_specs, check_vma=False)
```

time: 72.7 us -> 69.3 us (0.953)
  local copies, waits for them, and re-layouts: 4.91 us -> 0 us
  Pallas kernels: 66.3 us -> 67.8 us
    unnamed x13 -> x0, local copies, waits for them, and re-layouts: 4.91 us -> none
    pallas_call x1 -> x2, Pallas kernels: 66.3 us -> 67.8 us  [the longest x1 66 us: body(): pl.pallas_call(kernel, out_shape=outs, in_specs=[vmem, vmem, vmem, vmem,...]
where the time goes in v2:
time: 69.3 us; the launch traced here: 69.1 us
  Pallas kernels  67.8 us (98%)
  between operations  1.29 us (2%)
    pallas_call x1, Pallas kernels, body(): pl.pallas_call(kernel, out_shape=outs, in_specs=[vmem, vmem, vmem, vmem,...  66 us
    pallas_call x1, Pallas kernels, body(): pl.pallas_call(write_out, out_shape=outs, in_specs=[vmem] * 5, out_specs=...  1.86 us

profile of v2, /device:TPU:1, one launch (start us, length us, event | category | flops | bytes accessed | tf_op | source)
XLA Modules:
  0.0 69.1 jit_solution(10670221417961530448)
XLA Ops:
  1.3 66.0 %shard_map.110 = (f32[1,256]{1,0:T(1,128)}, f32[256,256]{1,0:T(8,128)}, f32[256,256]{1,0:T(8,128)}, f32[4,256]{1,0:T(4,128)}, f32[4,256]{1,0:T(4,128)}) custom-call(bf16[256,256]{1,0:T(8,128)(2,1)} %q_ref.1, bf16[256,256]{1,0:T(8,128)(2,1)} %c_ref.1, bf16[4,256]{1,0:T(4,128)(2,1)} %gq_ref.1, bf16[4,256]{1,0:T(4,128)(2,1)} %gc_ref.1, f32[8]{0:T(128)} %slope_ref.1, ...), custom_call_target="tpu_custom_call" | custom-call | tf_op jit(solution)/shard_map/pallas_call | solution.py:551
  67.3 1.9 %shard_map.111 = (f32[1,256]{1,0:T(1,128)}, f32[256,256]{1,0:T(8,128)}, f32[256,256]{1,0:T(8,128)}, f32[4,256]{1,0:T(4,128)}, f32[4,256]{1,0:T(4,128)}) custom-call(f32[1,256]{1,0:T(1,128)} %get-tuple-element.15.loss, f32[256,256]{1,0:T(8,128)} %get-tuple-element.16.ug, f32[256,256]{1,0:T(8,128)} %get-tuple-element.17.ig, f32[4,256]{1,0:T(4,128)} %get-tuple-element.18.ugate, ...), custom_call_target="tpu_custom_call" | custom-call | tf_op jit(solution)/shard_map/pallas_call | solution.py:561

commit v3 on v2

--- a/solution.py
+++ b/solution.py
@@ -16,6 +16,7 @@
 PIECES = ((0, 80), (80, 64))
 K = 8
 ROWS = 16
+BROWS = 32
 NT = (((1,), (1,)), ((), ()))
 
 
@@ -24,7 +25,7 @@
     loss_ref, ug_ref, ig_ref, ugate_ref, igate_ref,
     qall, ugall, call, xstage, gpad, git, ctall, qm, gub, tgtb,
     logit, weight, score, dinv, mx, sm, ps, stat, ltb,
-    lg, igp, ugv, uacc, ibk, sbuf, rbuf, gsend, grecv,
+    lg_a, lg_b, igp_a, igp_b, gacc, ugv, uacc, ib, qpair, sbuf, rbuf, gsend, grecv,
     urecv, ukeep, usend, uxrecv, isend, irecv, igx, ugsend, ugrecv,
     x_s, x_r, q_s, q_r, u_s, u_r, ag_s, ag_r, st_s, st_r,
     rs_s, rs_r, g_s, g_r, uc_s, uc_r, ux_s, ux_r, fx_s, fx_r, ugs_s, ugs_r,
@@ -97,7 +98,8 @@
     ps[...] = jnp.zeros_like(ps)
     uacc[...] = jnp.zeros_like(uacc)
     ugv[...] = jnp.zeros_like(ugv)
-    lg[1] = jnp.zeros((K, CH, US), BF16)
+    lg_b[...] = jnp.zeros_like(lg_b)
+    igp_b[...] = jnp.zeros_like(igp_b)
 
     x_item.wait_recv()
     for n in range(2):
@@ -110,9 +112,10 @@
 
     def mask_users(cc, h):
         for p in range(2):
+            rows = pl.ds(pl.multiple_of(cc * UB, UB), UB)
+            k = 4 * h + 2 * p
+            qpair[k // 2, rows, :] = qall[cc, h, :, p * CH : (p + 1) * CH]
             pair = qall[cc, h, :, p * CH : (p + 1) * CH].astype(F32)
-            k = 4 * h + 2 * p
-            rows = pl.ds(pl.multiple_of(cc * UB, UB), UB)
             qm[k, rows, :] = jnp.where(lane < 64, pair, 0.0).astype(BF16)
             qm[k + 1, rows, :] = jnp.where(lane < 64, 0.0, pair).astype(BF16)
 
@@ -133,16 +136,16 @@
         mask_users(1 - c, h)
 
     inv_t = 1.0 / jnp.full((8, US), t_ref[0], F32)
-    inv_t16 = jnp.concatenate([inv_t, inv_t], axis=0)
     scale2 = inv_t * LOG2E
-    row_iota = lax.broadcasted_iota(jnp.int32, (ROWS, US), 0)
 
     def twice(v):
         return jnp.concatenate([v, v], axis=0)
 
-    def is_positive(o, r):
-        ids = row_iota + ((o * 2 + c) * UB + x * CH + r * ROWS)
-        return twice(tgtb[...]) == ids.astype(F32)
+    def is_positive(o, r, rows):
+        ids = lax.broadcasted_iota(jnp.int32, (rows, US), 0) + (
+            (o * 2 + c) * UB + x * CH + r * rows
+        )
+        return jnp.concatenate([tgtb[...]] * (rows // 8), axis=0) == ids.astype(F32)
 
     def forward(j, carry):
         s = (j + 1) // 2
@@ -195,7 +198,7 @@
             sc = num * di
             dinv[o, rows, :] = di
             score[o, rows, :] = sc
-            hit = jnp.where(is_positive(o, r), sc, 0.0)
+            hit = jnp.where(is_positive(o, r, ROWS), sc, 0.0)
             return (
                 jnp.maximum(top, jnp.maximum(sc[:8], sc[8:])),
                 pos + hit[:8] + hit[8:],
@@ -243,8 +246,8 @@
     loss_ref[...] = jnp.where(jnp.broadcast_to(c, (1, UB)) == 0, loss[:, :UB], loss[:, UB:])
     ltb[...] = jnp.broadcast_to(log_total * LOG2E, (8, US))
 
-    ones_row = lax.broadcasted_iota(jnp.int32, (K, K * CH), 0)
-    ones_col = lax.broadcasted_iota(jnp.int32, (K, K * CH), 1) // CH
+    ones_row = lax.broadcasted_iota(jnp.int32, (8, 2 * CH), 0)
+    ones_col = lax.broadcasted_iota(jnp.int32, (8, 2 * CH), 1) // CH
     ones = jnp.where(ones_row == ones_col, 1.0, 0.0).astype(BF16)
 
     def gate_copy(dr, d):
@@ -268,32 +271,43 @@
             dev(z + 2 * dr - 1, c, h),
         )
 
-    def far_of(j):
-        d = 4 - (j + 1) // 2
-        return d, lax.rem(z + NZ + jnp.where(lax.rem(j, 2) == 1, -d, d), NZ)
-
-    def matmuls(o, b, k):
-        ibk[k] = jnp.dot(lg[b, k], qm[k], preferred_element_type=F32)
-        at = pl.ds(pl.multiple_of(k * 64, 64), 64)
-        part = jnp.dot(ctall[o, at, :], lg[b, k], preferred_element_type=F32)
-        uacc[0, at, :] += part[:, :UB]
-        uacc[1, at, :] += part[:, UB:]
+    def matmuls(o, lg, igp, r):
+        both = jnp.dot(
+            lg[pl.ds(pl.multiple_of(r * 2 * CH, 2 * CH), 2 * CH), :], qpair[r], preferred_element_type=F32
+        )
+        ib[r] = jnp.where(lane[:CH] < 64, both[:CH], both[CH:])
+        for kk in range(2):
+            at = pl.ds(pl.multiple_of(r * CH + kk * 64, 64), 64)
+            part = jnp.dot(
+                ctall[o, at, :],
+                lg[pl.ds(pl.multiple_of((2 * r + kk) * CH, CH), CH), :],
+                preferred_element_type=F32,
+            )
+            uacc[0, at, :] += part[:, :UB]
+            uacc[1, at, :] += part[:, UB:]
+        gates = igp[r]
+        hi = gates.astype(BF16)
+        lo = (gates - hi.astype(F32)).astype(BF16)
+        gacc[r] = lax.dot_general(ones, hi, NT, preferred_element_type=F32) + lax.dot_general(
+            ones, lo, NT, preferred_element_type=F32
+        )
 
     def item_sum(h):
-        return jnp.concatenate([ibk[4 * h] + ibk[4 * h + 1], ibk[4 * h + 2] + ibk[4 * h + 3]], axis=1)
-
-    def backward(j, carry):
-        d, o = far_of(j)
-        before = jnp.maximum(j - 1, 0)
-        d_before, o_before = far_of(before)
-        b = lax.rem(j, 2)
-
+        return jnp.concatenate([ib[2 * h], ib[2 * h + 1]], axis=1)
+
+    def gate_sum():
+        return jnp.concatenate([gacc[i, 0:2, :] for i in range(4)], axis=0)
+
+    def four(v):
+        return jnp.concatenate([v] * (BROWS // 8), axis=0)
+
+    def chunk(o, lg, igp, o_before, lg_before, igp_before):
         def rows_of(r, carry):
-            rows = pl.ds(pl.multiple_of(r * ROWS, ROWS), ROWS)
-            matmuls(o_before, 1 - b, r)
+            rows = pl.ds(pl.multiple_of(r * BROWS, BROWS), BROWS)
+            matmuls(o_before, lg_before, igp_before, r)
             sc = score[o, rows, :]
-            soft = jnp.exp2(sc * twice(scale2) - twice(ltb[...]))
-            soft = jnp.where(is_positive(o, r), soft - 1.0, soft) * inv_t16
+            soft = jnp.exp2(sc * four(scale2) - four(ltb[...]))
+            soft = jnp.where(is_positive(o, r, BROWS), soft - 1.0, soft) * four(inv_t)
             share = soft * dinv[o, rows, :]
             for k in range(K):
                 l = logit[o, k, rows, :]
@@ -302,87 +316,70 @@
                 gg = g * (l - sc)
                 sk = slope_ref[k]
                 out = g + gg * (sk - (t * t) * sk)
-                lg[b, k, rows, :] = out.astype(BF16)
-                ugv[k] = ugv[k] + (gg[:8] + gg[8:])
-                igp[rows, k * CH : (k + 1) * CH] = (gg[:, 0:128] + gg[:, 128:256]) + (
-                    gg[:, 256:384] + gg[:, 384:512]
-                )
+                lg[pl.ds(pl.multiple_of(k * CH + r * BROWS, BROWS), BROWS), :] = out.astype(BF16)
+                ugv[k] = ugv[k] + ((gg[:8] + gg[8:16]) + (gg[16:24] + gg[24:]))
+                igp[k // 2, rows, (k % 2) * CH : (k % 2 + 1) * CH] = (
+                    gg[:, 0:128] + gg[:, 128:256]
+                ) + (gg[:, 256:384] + gg[:, 384:512])
             return carry
 
-        lax.fori_loop(0, CH // ROWS, rows_of, 0)
-
-        dr_before = 1 - lax.rem(before, 2)
-
-        @pl.when(j == 1)
+        lax.fori_loop(0, CH // BROWS, rows_of, 0)
+
+    def send(dr, jj):
+        @pl.when(jj == 1)
+        def _():
+            for h in range(2):
+                sbuf[dr, 2, h] = item_sum(h).astype(BF16)
+                rs_copy(dr, 3, h).start()
+            gsend[dr, 2] = gate_sum()
+            gate_copy(dr, 3).start()
+
+        @pl.when(jj == 2)
+        def _():
+            for h in range(2):
+                rs_copy(dr, 3, h).wait_recv()
+                value = item_sum(h) + rbuf[dr, 2, h].astype(F32)
+                if h == dr:
+                    rs_copy(dr, 4, h).wait_recv()
+                    value = value + rbuf[dr, 3, h].astype(F32)
+                sbuf[dr, 1, h] = value.astype(BF16)
+                rs_copy(dr, 2, h).start()
+            gate_copy(dr, 3).wait_recv()
+            value = gate_sum() + grecv[dr, 2]
+            if dr == 0:
+                gate_copy(0, 4).wait_recv()
+                value = value + grecv[0, 3]
+            gsend[dr, 1] = value
+            gate_copy(dr, 2).start()
+
+        @pl.when(jj == 3)
+        def _():
+            for h in range(2):
+                sbuf[dr, 0, h] = item_sum(h).astype(BF16)
+            for w in (1, 0):
+                last_copy(dr, w).start()
+            gsend[dr, 0] = gate_sum()
+            gate_copy(dr, 1).start()
+
+    def backward(jj, carry):
+        d = 4 - jj
+        right = lax.rem(z + d, NZ)
+        chunk(right, lg_a, igp_a, lax.rem(z + NZ - d, NZ), lg_b, igp_b)
+        send(0, jj)
+        chunk(lax.rem(z + NZ - (d - 1), NZ), lg_b, igp_b, right, lg_a, igp_a)
+
+        @pl.when(jj == 0)
         def _():
             for h in range(2):
                 sbuf[h, 3, h] = item_sum(h).astype(BF16)
                 rs_copy(h, 4, h).start()
-
-        for dr in range(2):
-            mine = (j > 1) & (dr_before == dr)
-
-            @pl.when(mine & (d_before == 3))
-            def _():
-                for h in range(2):
-                    sbuf[dr, 2, h] = item_sum(h).astype(BF16)
-                    rs_copy(dr, 3, h).start()
-
-            @pl.when(mine & (d_before == 2))
-            def _():
-                for h in range(2):
-                    rs_copy(dr, 3, h).wait_recv()
-                    value = item_sum(h) + rbuf[dr, 2, h].astype(F32)
-                    if h == dr:
-                        rs_copy(dr, 4, h).wait_recv()
-                        value = value + rbuf[dr, 3, h].astype(F32)
-                    sbuf[dr, 1, h] = value.astype(BF16)
-                    rs_copy(dr, 2, h).start()
-
-            @pl.when(mine & (d_before == 1))
-            def _():
-                for h in range(2):
-                    sbuf[dr, 0, h] = item_sum(h).astype(BF16)
-                for w in (1, 0):
-                    last_copy(dr, w).start()
-
-        hi = igp[...].astype(BF16)
-        lo = (igp[...] - hi.astype(F32)).astype(BF16)
-        gate = lax.dot_general(ones, hi, NT, preferred_element_type=F32) + lax.dot_general(
-            ones, lo, NT, preferred_element_type=F32
-        )
-
-        @pl.when(j == 0)
-        def _():
-            gsend[0, 3] = gate
+            gsend[0, 3] = gate_sum()
             gate_copy(0, 4).start()
 
-        @pl.when(j == 7)
-        def _():
-            igx[0] = gate
-
-        for dr in range(2):
-            mine = (j > 0) & (j < 7) & (lax.rem(j, 2) == 1 - dr)
-            for dd in (1, 3):
-
-                @pl.when(mine & (d == dd))
-                def _():
-                    gsend[dr, dd - 1] = gate
-                    gate_copy(dr, dd).start()
-
-            @pl.when(mine & (d == 2))
-            def _():
-                gate_copy(dr, 3).wait_recv()
-                value = gate + grecv[dr, 2]
-                if dr == 0:
-                    gate_copy(0, 4).wait_recv()
-                    value = value + grecv[0, 3]
-                gsend[dr, 1] = value
-                gate_copy(dr, 2).start()
-
+        send(1, jj)
         return carry
 
-    lax.fori_loop(0, NZ, backward, 0)
+    lax.fori_loop(0, NZ // 2, backward, 0)
 
     for k in range(K):
         ugsend[k : k + 1, :] = jnp.sum(ugv[k], axis=0, keepdims=True)
@@ -406,9 +403,8 @@
 
     for hh in range(2):
         for p in range(2):
-            for kk in range(2):
-                h = 1 - x if hh == 0 else x
-                matmuls(z, 1, 4 * h + 2 * p + kk)
+            h = 1 - x if hh == 0 else x
+            matmuls(z, lg_b, igp_b, 2 * h + p)
             u_core(hh, p).start()
     for p in range(2):
         usend[p] = core_sum(0, p).astype(BF16)
@@ -425,7 +421,7 @@
     keep = jnp.where(first, sums[0], sums[1])
     i_x = rc(isend, irecv, fx_s.at[0], fx_r.at[0], xp)
     i_x.start()
-    gate = igx[0]
+    gate = gate_sum()
     for dr in range(2):
         for d in (2, 1):
             gate_copy(dr, d).wait_recv()
@@ -511,11 +507,15 @@
         pltpu.VMEM((8, US), F32),
         pltpu.VMEM((4, 8, US), F32),
         pltpu.VMEM((8, US), F32),
-        pltpu.VMEM((2, K, CH, US), BF16),
-        pltpu.VMEM((CH, K * CH), F32),
+        pltpu.VMEM((K * CH, US), BF16),
+        pltpu.VMEM((K * CH, US), BF16),
+        pltpu.VMEM((4, CH, 2 * CH), F32),
+        pltpu.VMEM((4, CH, 2 * CH), F32),
+        pltpu.VMEM((4, 8, CH), F32),
         pltpu.VMEM((K, 8, US), F32),
         pltpu.VMEM((2, US, UB), F32),
-        pltpu.VMEM((K, CH, CH), F32),
+        pltpu.VMEM((4, CH, CH), F32),
+        pltpu.VMEM((4, US, CH), BF16),
         pltpu.VMEM((2, 4, 2, CH, UB), BF16),
         pltpu.VMEM((2, 4, 2, CH, UB), BF16),
         pltpu.VMEM((2, 4, K, CH), F32),

time: 69.3 us -> 66.5 us (0.960)
  Pallas kernels: 67.8 us -> 65 us
    pallas_call x1, Pallas kernels: 66 us -> 63.1 us  [body(): pl.pallas_call(kernel, out_shape=outs, in_specs=[vmem, vmem, vmem, vmem,...]
where the time goes in v3:
time: 66.5 us; the launch traced here: 66.3 us
  Pallas kernels  65 us (98%)
  between operations  1.29 us (2%)
    pallas_call x1, Pallas kernels, body(): pl.pallas_call(kernel, out_shape=outs, in_specs=[vmem, vmem, vmem, vmem,...  63.1 us
    pallas_call x1, Pallas kernels, body(): pl.pallas_call(write_out, out_shape=outs, in_specs=[vmem] * 5, out_specs=...  1.86 us

profile of v3, /device:TPU:1, one launch (start us, length us, event | category | flops | bytes accessed | tf_op | source)
XLA Modules:
  0.0 66.3 jit_solution(6146979758123789298)
XLA Ops:
  1.3 63.1 %shard_map.110 = (f32[1,256]{1,0:T(1,128)}, f32[256,256]{1,0:T(8,128)}, f32[256,256]{1,0:T(8,128)}, f32[4,256]{1,0:T(4,128)}, f32[4,256]{1,0:T(4,128)}) custom-call(bf16[256,256]{1,0:T(8,128)(2,1)} %q_ref.1, bf16[256,256]{1,0:T(8,128)(2,1)} %c_ref.1, bf16[4,256]{1,0:T(4,128)(2,1)} %gq_ref.1, bf16[4,256]{1,0:T(4,128)(2,1)} %gc_ref.1, f32[8]{0:T(128)} %slope_ref.1, ...), custom_call_target="tpu_custom_call" | custom-call | tf_op jit(solution)/shard_map/pallas_call | solution.py:551
  64.4 1.9 %shard_map.111 = (f32[1,256]{1,0:T(1,128)}, f32[256,256]{1,0:T(8,128)}, f32[256,256]{1,0:T(8,128)}, f32[4,256]{1,0:T(4,128)}, f32[4,256]{1,0:T(4,128)}) custom-call(f32[1,256]{1,0:T(1,128)} %get-tuple-element.15.loss, f32[256,256]{1,0:T(8,128)} %get-tuple-element.16.ug, f32[256,256]{1,0:T(8,128)} %get-tuple-element.17.ig, f32[4,256]{1,0:T(4,128)} %get-tuple-element.18.ugate, ...), custom_call_target="tpu_custom_call" | custom-call | tf_op jit(solution)/shard_map/pallas_call | solution.py:561

commit v4 on v3

--- a/solution.py
+++ b/solution.py
@@ -23,8 +23,8 @@
 def kernel(
     q_ref, c_ref, gq_ref, gc_ref, slope_ref, t_ref, tgt_ref,
     loss_ref, ug_ref, ig_ref, ugate_ref, igate_ref,
-    qall, ugall, call, xstage, gpad, git, ctall, qm, gub, tgtb,
-    logit, weight, score, dinv, mx, sm, ps, stat, ltb,
+    qall, ugall, call, xstage, gpad_a, gpad_b, git_a, git_b, ctall, qm, gub, tgtb,
+    logit_a, logit_b, weight, score, dinv, mx, sm, ps, stat, ltb,
     lg_a, lg_b, igp_a, igp_b, gacc, ugv, uacc, ib, qpair, sbuf, rbuf, gsend, grecv,
     urecv, ukeep, usend, uxrecv, isend, irecv, igx, ugsend, ugrecv,
     x_s, x_r, q_s, q_r, u_s, u_r, ag_s, ag_r, st_s, st_r,
@@ -73,10 +73,22 @@
 
     def hop(dr, s, hh, n):
         step = 1 - 2 * dr
-        o = lax.rem(z - step * (s - 1) + NZ, NZ)
+        o = lax.rem(z - step * min(s - 1, 2) + NZ, NZ)
         h = x if hh == 0 else 1 - x
         at = call.at[o, h, pl.ds(*PIECES[n]), :]
-        return rc(at, at, ag_s.at[dr, s - 1, hh, n], ag_r.at[dr, s - 1, hh, n], dev(z + step, c, x))
+        return rc(at, at, ag_s.at[dr, s - 1, hh, n], ag_r.at[dr, s - 1, hh, n],
+                  dev(z + (2 * step if s == 4 else step), c, x))
+
+    def arrive(s, halves=(0, 1)):
+        for hh in halves:
+            for n in range(2):
+                for dr in range(2):
+                    if s < 4 or hh == dr:
+                        hop(dr, s, hh, n).wait_recv()
+                    if s == 2 and hh == dr:
+                        hop(dr, 4, hh, n).start()
+                    if s < 3:
+                        hop(dr, s + 1, hh, n).start()
 
     x_item = rc(xstage, call.at[z, x], x_s.at[0], x_r.at[0], xp)
     q_x = rc(q_ref, qall.at[c, x], q_s.at[0], q_r.at[0], xp)
@@ -92,7 +104,8 @@
         s.start()
     q_c.start()
 
-    gpad[...] = jnp.zeros_like(gpad)
+    gpad_a[...] = jnp.zeros_like(gpad_a)
+    gpad_b[...] = jnp.zeros_like(gpad_b)
     mx[...] = jnp.full(mx.shape, -3.0e38, F32)
     sm[...] = jnp.zeros_like(sm)
     ps[...] = jnp.zeros_like(ps)
@@ -107,6 +120,7 @@
         hop(1, 1, 1, n).start()
     q_x.wait_recv()
     q_f.start()
+    arrive(1, (0,))
 
     lane = lax.broadcasted_iota(jnp.int32, (UB, CH), 1)
 
@@ -147,34 +161,18 @@
         )
         return jnp.concatenate([tgtb[...]] * (rows // 8), axis=0) == ids.astype(F32)
 
-    def forward(j, carry):
-        s = (j + 1) // 2
-        odd = lax.rem(j, 2) == 1
-
-        @pl.when(odd)
-        def _():
-            for hh in range(2):
-                for n in range(2):
-                    for dr in range(2):
-                        last = 4 if hh == dr else 3
-
-                        @pl.when(s <= last)
-                        def _():
-                            hop(dr, s, hh, n).wait_recv()
-
-                        @pl.when(s < last)
-                        def _():
-                            hop(dr, s + 1, hh, n).start()
-
-        o = lax.rem(z + NZ + jnp.where(odd, -s, s), NZ)
+    def gates_of(o, gpad, git):
         gpad[0:16, :] = call[o, 0, CH:, :CH].astype(F32)
         gpad[16:32, :] = call[o, 1, CH:, :CH].astype(F32)
         git[...] = gpad[...].T * LOG2E
-        for k in range(K):
-            h, p = k // 4, (k % 4) // 2
-            logit[o, k] = lax.dot_general(
-                call[o, h, :CH, p * CH : (p + 1) * CH], qm[k], NT, preferred_element_type=F32
-            )
+
+    def logits_of(o, logit, s, k):
+        h, p = k // 4, lax.rem(k, 4) // 2
+        at = pl.ds(pl.multiple_of(p * CH, CH), CH)
+        logit[s, k] = lax.dot_general(call[o, h, :CH, at], qm[k], NT, preferred_element_type=F32)
+
+    def scores_of(o, logit, s, git, o_next, logit_next, s_next, gpad_next, git_next):
+        gates_of(o_next, gpad_next, git_next)
         for h in range(2):
             for p in range(2):
                 at = slice((2 * h + p) * CH, (2 * h + p + 1) * CH)
@@ -182,12 +180,13 @@
 
         def rows_of(r, carry):
             top, pos = carry
+            logits_of(o_next, logit_next, s_next, r)
             rows = pl.ds(pl.multiple_of(r * ROWS, ROWS), ROWS)
             den = num = None
             gcols = git[rows, :]
             for k in range(K):
                 col = (k // 4) * 16 + k % 4
-                l = logit[o, k, rows, :]
+                l = logit[s, k, rows, :]
                 e = jnp.tanh(l) * (slope_ref[k] * LOG2E) + gcols[:, col : col + 1] + twice(gub[k])
                 w = jnp.exp2(e)
                 weight[o, k, rows, :] = w
@@ -205,7 +204,7 @@
             )
 
         before = mx[...]
-        top, pos = lax.fori_loop(0, CH // ROWS, rows_of, (before, ps[...]))
+        top, pos = lax.fori_loop(0, CH // ROWS, rows_of, (before, ps[...]), unroll=True)
         mx[...] = top
         ps[...] = pos
         shift = top * scale2
@@ -213,9 +212,33 @@
         for m in range(CH // 8):
             total = total + jnp.exp2(score[o, m * 8 : (m + 1) * 8, :] * scale2 - shift)
         sm[...] = total
+
+    arrive(1, (1,))
+    gates_of(z, gpad_a, git_a)
+
+    def own_logits(k, carry):
+        logits_of(z, logit_a, 0, k)
         return carry
 
-    lax.fori_loop(0, NZ, forward, 0)
+    lax.fori_loop(0, K, own_logits, 0, unroll=True)
+
+    def forward(i, carry):
+        for s in (2, 3, 4):
+
+            @pl.when(i == s - 1)
+            def _():
+                arrive(s)
+
+        left = lax.rem(z + NZ - i, NZ)
+        right = lax.rem(z + i + 1, NZ)
+        after = jnp.minimum(i + 1, 3)
+        scores_of(left, logit_a, i, git_a, right, logit_b, i, gpad_b, git_b)
+        scores_of(
+            right, logit_b, i, git_b, lax.rem(z + NZ - after, NZ), logit_a, after, gpad_a, git_a
+        )
+        return carry
+
+    lax.fori_loop(0, NZ // 2, forward, 0)
 
     top = jnp.max(mx[...], axis=0, keepdims=True)
     total = sm[...] * jnp.exp2((mx[...] - top) * scale2)
@@ -251,14 +274,14 @@
     ones = jnp.where(ones_row == ones_col, 1.0, 0.0).astype(BF16)
 
     def gate_copy(dr, d):
-        far = 2 if d in (2, 4) else 1
+        far = 2 if d == 4 else 1
         return rc(
             gsend.at[dr, d - 1], grecv.at[dr, d - 1], g_s.at[dr, d - 1], g_r.at[dr, d - 1],
             dev(z + far * (2 * dr - 1), c, x),
         )
 
     def rs_copy(dr, d, h):
-        far = 2 if d in (2, 4) else 1
+        far = 2 if d == 4 else 1
         return rc(
             sbuf.at[dr, d - 1, h], rbuf.at[dr, d - 1, h], rs_s.at[dr, d - 1, h], rs_r.at[dr, d - 1, h],
             dev(z + far * (2 * dr - 1), c, x),
@@ -301,7 +324,7 @@
     def four(v):
         return jnp.concatenate([v] * (BROWS // 8), axis=0)
 
-    def chunk(o, lg, igp, o_before, lg_before, igp_before):
+    def chunk(o, logit, s, lg, igp, o_before, lg_before, igp_before):
         def rows_of(r, carry):
             rows = pl.ds(pl.multiple_of(r * BROWS, BROWS), BROWS)
             matmuls(o_before, lg_before, igp_before, r)
@@ -310,7 +333,7 @@
             soft = jnp.where(is_positive(o, r, BROWS), soft - 1.0, soft) * four(inv_t)
             share = soft * dinv[o, rows, :]
             for k in range(K):
-                l = logit[o, k, rows, :]
+                l = logit[s, k, rows, :]
                 t = jnp.tanh(l)
                 g = weight[o, k, rows, :] * share
                 gg = g * (l - sc)
@@ -323,7 +346,7 @@
                 ) + (gg[:, 256:384] + gg[:, 384:512])
             return carry
 
-        lax.fori_loop(0, CH // BROWS, rows_of, 0)
+        lax.fori_loop(0, CH // BROWS, rows_of, 0, unroll=True)
 
     def send(dr, jj):
         @pl.when(jj == 1)
@@ -355,18 +378,20 @@
         @pl.when(jj == 3)
         def _():
             for h in range(2):
-                sbuf[dr, 0, h] = item_sum(h).astype(BF16)
+                rs_copy(dr, 2, h).wait_recv()
+                sbuf[dr, 0, h] = (item_sum(h) + rbuf[dr, 1, h].astype(F32)).astype(BF16)
             for w in (1, 0):
                 last_copy(dr, w).start()
-            gsend[dr, 0] = gate_sum()
+            gate_copy(dr, 2).wait_recv()
+            gsend[dr, 0] = gate_sum() + grecv[dr, 1]
             gate_copy(dr, 1).start()
 
     def backward(jj, carry):
         d = 4 - jj
         right = lax.rem(z + d, NZ)
-        chunk(right, lg_a, igp_a, lax.rem(z + NZ - d, NZ), lg_b, igp_b)
+        chunk(right, logit_b, d - 1, lg_a, igp_a, lax.rem(z + NZ - d, NZ), lg_b, igp_b)
         send(0, jj)
-        chunk(lax.rem(z + NZ - (d - 1), NZ), lg_b, igp_b, right, lg_a, igp_a)
+        chunk(lax.rem(z + NZ - (d - 1), NZ), logit_a, d - 1, lg_b, igp_b, right, lg_a, igp_a)
 
         @pl.when(jj == 0)
         def _():
@@ -410,12 +435,7 @@
         usend[p] = core_sum(0, p).astype(BF16)
         u_x(p).start()
 
-    def own_sum(h):
-        for dr in range(2):
-            rs_copy(dr, 2, h).wait_recv()
-        return item_sum(h) + (rbuf[0, 1, h].astype(F32) + rbuf[1, 1, h].astype(F32))
-
-    sums = [own_sum(h) for h in range(2)]
+    sums = [item_sum(h) for h in range(2)]
     first = jnp.broadcast_to(x, (CH, UB)) == 0
     isend[...] = jnp.where(first, sums[1], sums[0]).astype(BF16)
     keep = jnp.where(first, sums[0], sums[1])
@@ -423,9 +443,8 @@
     i_x.start()
     gate = gate_sum()
     for dr in range(2):
-        for d in (2, 1):
-            gate_copy(dr, d).wait_recv()
-            gate = gate + grecv[dr, d - 1]
+        gate_copy(dr, 1).wait_recv()
+        gate = gate + grecv[dr, 0]
     igx[0] = gate
     ig_x = rc(igx.at[0], igx.at[1], fx_s.at[1], fx_r.at[1], xp)
     ig_x.start()
@@ -494,11 +513,14 @@
         pltpu.VMEM((SLOT, UB), BF16),
         pltpu.VMEM((CH, CH), F32),
         pltpu.VMEM((CH, CH), F32),
+        pltpu.VMEM((CH, CH), F32),
+        pltpu.VMEM((CH, CH), F32),
         pltpu.VMEM((NZ, K * 64, CH), BF16),
         pltpu.VMEM((K, US, CH), BF16),
         pltpu.VMEM((K, 8, US), F32),
         pltpu.VMEM((8, US), F32),
-        pltpu.VMEM((NZ, K, CH, US), F32),
+        pltpu.VMEM((NZ // 2, K, CH, US), F32),
+        pltpu.VMEM((NZ // 2, K, CH, US), F32),
         pltpu.VMEM((NZ, K, CH, US), F32),
         pltpu.VMEM((NZ, CH, US), F32),
         pltpu.VMEM((NZ, CH, US), F32),

time: 66.5 us -> 66 us (level)
  no operation moved by 1% of the time
where the time goes in v4:
time: 66 us; the launch traced here: 65.9 us
  Pallas kernels  64.6 us (98%)
  between operations  1.29 us (2%)
    pallas_call x1, Pallas kernels, body(): pl.pallas_call(kernel, out_shape=outs, in_specs=[vmem, vmem, vmem, vmem,...  62.7 us
    pallas_call x1, Pallas kernels, body(): pl.pallas_call(write_out, out_shape=outs, in_specs=[vmem] * 5, out_specs=...  1.86 us

profile of v4, /device:TPU:1, one launch (start us, length us, event | category | flops | bytes accessed | tf_op | source)
XLA Modules:
  0.0 65.9 jit_solution(11255657178547281900)
XLA Ops:
  1.3 62.7 %shard_map.110 = (f32[1,256]{1,0:T(1,128)}, f32[256,256]{1,0:T(8,128)}, f32[256,256]{1,0:T(8,128)}, f32[4,256]{1,0:T(4,128)}, f32[4,256]{1,0:T(4,128)}) custom-call(bf16[256,256]{1,0:T(8,128)(2,1)} %q_ref.1, bf16[256,256]{1,0:T(8,128)(2,1)} %c_ref.1, bf16[4,256]{1,0:T(4,128)(2,1)} %gq_ref.1, bf16[4,256]{1,0:T(4,128)(2,1)} %gc_ref.1, f32[8]{0:T(128)} %slope_ref.1, ...), custom_call_target="tpu_custom_call" | custom-call | tf_op jit(solution)/shard_map/pallas_call | solution.py:573
  64.0 1.9 %shard_map.111 = (f32[1,256]{1,0:T(1,128)}, f32[256,256]{1,0:T(8,128)}, f32[256,256]{1,0:T(8,128)}, f32[4,256]{1,0:T(4,128)}, f32[4,256]{1,0:T(4,128)}) custom-call(f32[1,256]{1,0:T(1,128)} %get-tuple-element.15.loss, f32[256,256]{1,0:T(8,128)} %get-tuple-element.16.ug, f32[256,256]{1,0:T(8,128)} %get-tuple-element.17.ig, f32[4,256]{1,0:T(4,128)} %get-tuple-element.18.ugate, ...), custom_call_target="tpu_custom_call" | custom-call | tf_op jit(solution)/shard_map/pallas_call | solution.py:583

commit v5 on v4

--- a/solution.py
+++ b/solution.py
@@ -25,8 +25,8 @@
     loss_ref, ug_ref, ig_ref, ugate_ref, igate_ref,
     qall, ugall, call, xstage, gpad_a, gpad_b, git_a, git_b, ctall, qm, gub, tgtb,
     logit_a, logit_b, weight, score, dinv, mx, sm, ps, stat, ltb,
-    lg_a, lg_b, igp_a, igp_b, gacc, ugv, uacc, ib, qpair, sbuf, rbuf, gsend, grecv,
-    urecv, ukeep, usend, uxrecv, isend, irecv, igx, ugsend, ugrecv,
+    lg_a, lg_b, igp_a, igp_b, gacc_a, gacc_b, gacc_c, ugv, uacc, ib_a, ib_b, ib_c, qpair, sbuf, rbuf, gsend, grecv,
+    urecv, ukeep, usend, uxrecv, isend, irecv, keep, igx, ugsend, ugrecv,
     x_s, x_r, q_s, q_r, u_s, u_r, ag_s, ag_r, st_s, st_r,
     rs_s, rs_r, g_s, g_r, uc_s, uc_r, ux_s, ux_r, fx_s, fx_r, ugs_s, ugs_r,
 ):
@@ -48,7 +48,7 @@
     quad = (xp, cp, dp)
 
     barrier = pltpu.get_barrier_semaphore()
-    near = [dev(z + d, c, x) for d in (-2, -1, 1, 2)] + [dev(z + d, c, 1 - x) for d in (-1, 1)]
+    near = [dev(z + d, c, x) for d in (-2, -1, 1, 2, 4)] + [dev(z + d, c, 1 - x) for d in (-1, 1, 4)]
     for peer in (*quad, *near):
         pl.semaphore_signal(barrier, inc=1, device_id=peer, device_id_type=MESH)
 
@@ -274,17 +274,23 @@
     ones = jnp.where(ones_row == ones_col, 1.0, 0.0).astype(BF16)
 
     def gate_copy(dr, d):
-        far = 2 if d == 4 else 1
+        far = 4 if d == 4 else 1
         return rc(
             gsend.at[dr, d - 1], grecv.at[dr, d - 1], g_s.at[dr, d - 1], g_r.at[dr, d - 1],
             dev(z + far * (2 * dr - 1), c, x),
         )
 
     def rs_copy(dr, d, h):
-        far = 2 if d == 4 else 1
+        far = 4 if d == 4 else 1
         return rc(
             sbuf.at[dr, d - 1, h], rbuf.at[dr, d - 1, h], rs_s.at[dr, d - 1, h], rs_r.at[dr, d - 1, h],
             dev(z + far * (2 * dr - 1), c, x),
+        )
+
+    def far_copy(w):
+        h = x if w == 0 else 1 - x
+        return rc(
+            sbuf.at[0, 3, h], rbuf.at[0, 3, w], rs_s.at[0, 3, w], rs_r.at[0, 3, w], dev(z + 4, c, h)
         )
 
     def last_copy(dr, w):
@@ -294,7 +300,7 @@
             dev(z + 2 * dr - 1, c, h),
         )
 
-    def matmuls(o, lg, igp, r):
+    def matmuls(o, lg, igp, ib, gacc, r):
         both = jnp.dot(
             lg[pl.ds(pl.multiple_of(r * 2 * CH, 2 * CH), 2 * CH), :], qpair[r], preferred_element_type=F32
         )
@@ -315,19 +321,19 @@
             ones, lo, NT, preferred_element_type=F32
         )
 
-    def item_sum(h):
+    def item_sum(ib, h):
         return jnp.concatenate([ib[2 * h], ib[2 * h + 1]], axis=1)
 
-    def gate_sum():
+    def gate_sum(gacc):
         return jnp.concatenate([gacc[i, 0:2, :] for i in range(4)], axis=0)
 
     def four(v):
         return jnp.concatenate([v] * (BROWS // 8), axis=0)
 
-    def chunk(o, logit, s, lg, igp, o_before, lg_before, igp_before):
+    def chunk(o, logit, s, lg, igp, o_before, lg_before, igp_before, ib, gacc):
         def rows_of(r, carry):
             rows = pl.ds(pl.multiple_of(r * BROWS, BROWS), BROWS)
-            matmuls(o_before, lg_before, igp_before, r)
+            matmuls(o_before, lg_before, igp_before, ib, gacc, r)
             sc = score[o, rows, :]
             soft = jnp.exp2(sc * four(scale2) - four(ltb[...]))
             soft = jnp.where(is_positive(o, r, BROWS), soft - 1.0, soft) * four(inv_t)
@@ -348,100 +354,112 @@
 
         lax.fori_loop(0, CH // BROWS, rows_of, 0, unroll=True)
 
-    def send(dr, jj):
-        @pl.when(jj == 1)
-        def _():
+    def send(dr, d, ib, gacc):
+        if d == 3:
             for h in range(2):
-                sbuf[dr, 2, h] = item_sum(h).astype(BF16)
+                sbuf[dr, 2, h] = item_sum(ib, h).astype(BF16)
                 rs_copy(dr, 3, h).start()
-            gsend[dr, 2] = gate_sum()
+            gsend[dr, 2] = gate_sum(gacc)
             gate_copy(dr, 3).start()
-
-        @pl.when(jj == 2)
-        def _():
+        elif d == 2:
             for h in range(2):
                 rs_copy(dr, 3, h).wait_recv()
-                value = item_sum(h) + rbuf[dr, 2, h].astype(F32)
-                if h == dr:
-                    rs_copy(dr, 4, h).wait_recv()
-                    value = value + rbuf[dr, 3, h].astype(F32)
+                value = item_sum(ib, h) + rbuf[dr, 2, h].astype(F32)
                 sbuf[dr, 1, h] = value.astype(BF16)
                 rs_copy(dr, 2, h).start()
             gate_copy(dr, 3).wait_recv()
-            value = gate_sum() + grecv[dr, 2]
-            if dr == 0:
-                gate_copy(0, 4).wait_recv()
-                value = value + grecv[0, 3]
-            gsend[dr, 1] = value
+            gsend[dr, 1] = gate_sum(gacc) + grecv[dr, 2]
             gate_copy(dr, 2).start()
+        else:
+            for h in range(2):
+                rs_copy(dr, 2, h).wait_recv()
+                sbuf[dr, 0, h] = (item_sum(ib, h) + rbuf[dr, 1, h].astype(F32)).astype(BF16)
+            for w in (1, 0):
+                last_copy(dr, w).start()
+            gate_copy(dr, 2).wait_recv()
+            gsend[dr, 0] = gate_sum(gacc) + grecv[dr, 1]
+            gate_copy(dr, 1).start()
+
+    first = jnp.broadcast_to(x, (CH, UB)) == 0
+    i_x = rc(isend, irecv, fx_s.at[0], fx_r.at[0], xp)
+
+    def backward(jj, carry):
+        a = jnp.where(jj == 0, 3, jnp.where(jj == 1, 0, 4 - jj))
+        b = jnp.where(jj == 2, 3, jnp.where(jj == 3, 0, 2 - jj))
+        b_before = jnp.where(jj == 3, 3, 3 - jj)
+        left = lax.rem(z + NZ - a, NZ)
+        right = lax.rem(z + b + 1, NZ)
+        right_before = lax.rem(z + lax.rem(b_before, 4) + 1, NZ)
+        chunk(left, logit_a, a, lg_a, igp_a, right_before, lg_b, igp_b, ib_a, gacc_a)
+
+        @pl.when(jj == 1)
+        def _():
+            send(1, 3, ib_a, gacc_a)
 
         @pl.when(jj == 3)
         def _():
             for h in range(2):
-                rs_copy(dr, 2, h).wait_recv()
-                sbuf[dr, 0, h] = (item_sum(h) + rbuf[dr, 1, h].astype(F32)).astype(BF16)
-            for w in (1, 0):
-                last_copy(dr, w).start()
-            gate_copy(dr, 2).wait_recv()
-            gsend[dr, 0] = gate_sum() + grecv[dr, 1]
-            gate_copy(dr, 1).start()
-
-    def backward(jj, carry):
-        d = 4 - jj
-        right = lax.rem(z + d, NZ)
-        chunk(right, logit_b, d - 1, lg_a, igp_a, lax.rem(z + NZ - d, NZ), lg_b, igp_b)
-        send(0, jj)
-        chunk(lax.rem(z + NZ - (d - 1), NZ), logit_a, d - 1, lg_b, igp_b, right, lg_a, igp_a)
+                sbuf[0, 3, h] = item_sum(ib_a, h).astype(BF16)
+            for w in range(2):
+                far_copy(w).start()
+            gsend[0, 3] = gate_sum(gacc_a)
+            gate_copy(0, 4).start()
+
+        chunk(right, logit_b, b, lg_b, igp_b, left, lg_a, igp_a, ib_b, gacc_b)
 
         @pl.when(jj == 0)
         def _():
-            for h in range(2):
-                sbuf[h, 3, h] = item_sum(h).astype(BF16)
-                rs_copy(h, 4, h).start()
-            gsend[0, 3] = gate_sum()
-            gate_copy(0, 4).start()
-
-        send(1, jj)
+            send(0, 3, ib_b, gacc_b)
+
+        @pl.when(jj == 1)
+        def _():
+            sums = [item_sum(ib_b, h) for h in range(2)]
+            isend[...] = jnp.where(first, sums[1], sums[0]).astype(BF16)
+            keep[...] = jnp.where(first, sums[0], sums[1])
+            i_x.start()
+            igx[0] = gate_sum(gacc_b)
+
+        @pl.when(jj == 2)
+        def _():
+            send(0, 2, ib_b, gacc_b)
+            send(1, 2, ib_a, gacc_a)
+
         return carry
 
     lax.fori_loop(0, NZ // 2, backward, 0)
+
+    def u_core(hh, p):
+        h = 1 - x if hh == 0 else x
+        at = pl.ds(pl.multiple_of(h * UB + p * CH, CH), CH)
+        return rc(uacc.at[1 - c, at, :], urecv.at[hh, p], uc_s.at[hh, p], uc_r.at[hh, p], cp)
+
+    def u_x(p):
+        return rc(usend.at[p], uxrecv.at[p], ux_s.at[p], ux_r.at[p], xp)
+
+    def core_sum(hh, p):
+        h = 1 - x if hh == 0 else x
+        at = pl.ds(pl.multiple_of(h * UB + p * CH, CH), CH)
+        u_core(hh, p).wait_recv()
+        return uacc[c, at, :] + urecv[hh, p]
+
+    for hh in range(2):
+        for p in range(2):
+            h = 1 - x if hh == 0 else x
+            matmuls(lax.rem(z + 1, NZ), lg_b, igp_b, ib_c, gacc_c, 2 * h + p)
+            u_core(hh, p).start()
+    send(0, 1, ib_b, gacc_b)
+    send(1, 1, ib_c, gacc_c)
+    for p in range(2):
+        usend[p] = core_sum(0, p).astype(BF16)
+        u_x(p).start()
 
     for k in range(K):
         ugsend[k : k + 1, :] = jnp.sum(ugv[k], axis=0, keepdims=True)
     ug_sends = [rc(ugsend, ugrecv.at[i], ugs_s.at[i], ugs_r.at[i], quad[i]) for i in range(3)]
     for s in ug_sends:
         s.start()
-
-    def u_core(hh, p):
-        h = 1 - x if hh == 0 else x
-        at = pl.ds(pl.multiple_of(h * UB + p * CH, CH), CH)
-        return rc(uacc.at[1 - c, at, :], urecv.at[hh, p], uc_s.at[hh, p], uc_r.at[hh, p], cp)
-
-    def u_x(p):
-        return rc(usend.at[p], uxrecv.at[p], ux_s.at[p], ux_r.at[p], xp)
-
-    def core_sum(hh, p):
-        h = 1 - x if hh == 0 else x
-        at = pl.ds(pl.multiple_of(h * UB + p * CH, CH), CH)
-        u_core(hh, p).wait_recv()
-        return uacc[c, at, :] + urecv[hh, p]
-
-    for hh in range(2):
-        for p in range(2):
-            h = 1 - x if hh == 0 else x
-            matmuls(z, lg_b, igp_b, 2 * h + p)
-            u_core(hh, p).start()
-    for p in range(2):
-        usend[p] = core_sum(0, p).astype(BF16)
-        u_x(p).start()
-
-    sums = [item_sum(h) for h in range(2)]
-    first = jnp.broadcast_to(x, (CH, UB)) == 0
-    isend[...] = jnp.where(first, sums[1], sums[0]).astype(BF16)
-    keep = jnp.where(first, sums[0], sums[1])
-    i_x = rc(isend, irecv, fx_s.at[0], fx_r.at[0], xp)
-    i_x.start()
-    gate = gate_sum()
+    gate_copy(0, 4).wait_recv()
+    gate = igx[0] + grecv[0, 3]
     for dr in range(2):
         gate_copy(dr, 1).wait_recv()
         gate = gate + grecv[dr, 0]
@@ -457,13 +475,17 @@
     ugate = jnp.where(jnp.broadcast_to(c, (K, UB)) == 0, ugate[:, :UB], ugate[:, UB:])
     ugate_ref[...] = jnp.where(jnp.broadcast_to(x, (4, UB)) == 0, ugate[:4], ugate[4:])
 
+    for w in range(2):
+        far_copy(w).wait_recv()
     for dr in range(2):
         last_copy(dr, 0).wait_recv()
-    ig_ref[own_rows, :] = keep + (rbuf[0, 0, 0].astype(F32) + rbuf[1, 0, 0].astype(F32))
+    ig_ref[own_rows, :] = (keep[...] + rbuf[0, 3, 0].astype(F32)) + (
+        rbuf[0, 0, 0].astype(F32) + rbuf[1, 0, 0].astype(F32)
+    )
     for dr in range(2):
         last_copy(dr, 1).wait_recv()
     i_x.wait_recv()
-    ig_ref[peer_rows, :] = irecv[...].astype(F32) + (
+    ig_ref[peer_rows, :] = (irecv[...].astype(F32) + rbuf[0, 3, 1].astype(F32)) + (
         rbuf[0, 0, 1].astype(F32) + rbuf[1, 0, 1].astype(F32)
     )
     ig_x.wait_recv()
@@ -484,7 +506,7 @@
             u_core(hh, p).wait_send()
     gate_copy(0, 4).wait_send()
     for dr in range(2):
-        rs_copy(dr, 4, dr).wait_send()
+        far_copy(dr).wait_send()
         for d in (1, 2, 3):
             gate_copy(dr, d).wait_send()
         for w in range(2):
@@ -534,8 +556,12 @@
         pltpu.VMEM((4, CH, 2 * CH), F32),
         pltpu.VMEM((4, CH, 2 * CH), F32),
         pltpu.VMEM((4, 8, CH), F32),
+        pltpu.VMEM((4, 8, CH), F32),
+        pltpu.VMEM((4, 8, CH), F32),
         pltpu.VMEM((K, 8, US), F32),
         pltpu.VMEM((2, US, UB), F32),
+        pltpu.VMEM((4, CH, CH), F32),
+        pltpu.VMEM((4, CH, CH), F32),
         pltpu.VMEM((4, CH, CH), F32),
         pltpu.VMEM((4, US, CH), BF16),
         pltpu.VMEM((2, 4, 2, CH, UB), BF16),
@@ -548,6 +574,7 @@
         pltpu.VMEM((2, CH, UB), BF16),
         pltpu.VMEM((CH, UB), BF16),
         pltpu.VMEM((CH, UB), BF16),
+        pltpu.VMEM((CH, UB), F32),
         pltpu.VMEM((2, K, CH), F32),
         pltpu.VMEM((K, US), F32),
         pltpu.VMEM((3, K, US), F32),

time: 66 us -> 67.7 us (1.026)
  Pallas kernels: 64.6 us -> 66.3 us
    pallas_call x1, Pallas kernels: 62.7 us -> 64.4 us  [body(): pl.pallas_call(kernel, out_shape=outs, in_specs=[vmem, vmem, vmem, vmem,...]
where the time goes in v5:
time: 67.7 us; the launch traced here: 67.6 us
  Pallas kernels  66.3 us (98%)
  between operations  1.29 us (2%)
    pallas_call x1, Pallas kernels, body(): pl.pallas_call(kernel, out_shape=outs, in_specs=[vmem, vmem, vmem, vmem,...  64.4 us
    pallas_call x1, Pallas kernels, body(): pl.pallas_call(write_out, out_shape=outs, in_specs=[vmem] * 5, out_specs=...  1.86 us

profile of v5, /device:TPU:1, one launch (start us, length us, event | category | flops | bytes accessed | tf_op | source)
XLA Modules:
  0.0 67.6 jit_solution(4638545486790102496)
XLA Ops:
  1.3 64.4 %shard_map.110 = (f32[1,256]{1,0:T(1,128)}, f32[256,256]{1,0:T(8,128)}, f32[256,256]{1,0:T(8,128)}, f32[4,256]{1,0:T(4,128)}, f32[4,256]{1,0:T(4,128)}) custom-call(bf16[256,256]{1,0:T(8,128)(2,1)} %q_ref.1, bf16[256,256]{1,0:T(8,128)(2,1)} %c_ref.1, bf16[4,256]{1,0:T(4,128)(2,1)} %gq_ref.1, bf16[4,256]{1,0:T(4,128)(2,1)} %gc_ref.1, f32[8]{0:T(128)} %slope_ref.1, ...), custom_call_target="tpu_custom_call" | custom-call | tf_op jit(solution)/shard_map/pallas_call | solution.py:600
  65.7 1.9 %shard_map.111 = (f32[1,256]{1,0:T(1,128)}, f32[256,256]{1,0:T(8,128)}, f32[256,256]{1,0:T(8,128)}, f32[4,256]{1,0:T(4,128)}, f32[4,256]{1,0:T(4,128)}) custom-call(f32[1,256]{1,0:T(1,128)} %get-tuple-element.15.loss, f32[256,256]{1,0:T(8,128)} %get-tuple-element.16.ug, f32[256,256]{1,0:T(8,128)} %get-tuple-element.17.ig, f32[4,256]{1,0:T(4,128)} %get-tuple-element.18.ugate, ...), custom_call_target="tpu_custom_call" | custom-call | tf_op jit(solution)/shard_map/pallas_call | solution.py:610

commit v6 on v4

--- a/solution.py
+++ b/solution.py
@@ -25,7 +25,7 @@
     loss_ref, ug_ref, ig_ref, ugate_ref, igate_ref,
     qall, ugall, call, xstage, gpad_a, gpad_b, git_a, git_b, ctall, qm, gub, tgtb,
     logit_a, logit_b, weight, score, dinv, mx, sm, ps, stat, ltb,
-    lg_a, lg_b, igp_a, igp_b, gacc, ugv, uacc, ib, qpair, sbuf, rbuf, gsend, grecv,
+    lg_a, lg_b, igp_a, igp_b, gacc_a, gacc_b, gacc_c, ugv, uacc, ib_a, ib_b, ib_c, qpair, sbuf, rbuf, gsend, grecv,
     urecv, ukeep, usend, uxrecv, isend, irecv, igx, ugsend, ugrecv,
     x_s, x_r, q_s, q_r, u_s, u_r, ag_s, ag_r, st_s, st_r,
     rs_s, rs_r, g_s, g_r, uc_s, uc_r, ux_s, ux_r, fx_s, fx_r, ugs_s, ugs_r,
@@ -90,16 +90,23 @@
                     if s < 3:
                         hop(dr, s + 1, hh, n).start()
 
-    x_item = rc(xstage, call.at[z, x], x_s.at[0], x_r.at[0], xp)
-    q_x = rc(q_ref, qall.at[c, x], q_s.at[0], q_r.at[0], xp)
-    q_c = rc(q_ref, qall.at[c, x], q_s.at[1], q_r.at[1], cp)
-    q_f = rc(qall.at[c, 1 - x], qall.at[c, 1 - x], q_s.at[2], q_r.at[2], cp)
+    x_items, q_xs, q_fs = [], [], []
+    for n in range(2):
+        part = pl.ds(*PIECES[n])
+        x_items.append(rc(xstage.at[part, :], call.at[z, x, part, :], x_s.at[n], x_r.at[n], xp))
+        part = pl.ds(n * CH, CH)
+        q_xs.append(rc(q_ref.at[part, :], qall.at[c, x, part, :], q_s.at[n], q_r.at[n], xp))
+        come = qall.at[c, 1 - x, part, :]
+        q_fs.append(rc(come, come, q_s.at[3 + n], q_r.at[3 + n], cp))
+    q_c = rc(q_ref, qall.at[c, x], q_s.at[2], q_r.at[2], cp)
     u_sends = [rc(ugall.at[me], ugall.at[me], u_s.at[i], u_r.at[i], quad[i]) for i in range(3)]
-    x_item.start()
+    for copy in x_items:
+        copy.start()
     for n in range(2):
         hop(0, 1, 0, n).start()
         hop(1, 1, 0, n).start()
-    q_x.start()
+    for copy in q_xs:
+        copy.start()
     for s in u_sends:
         s.start()
     q_c.start()
@@ -114,12 +121,13 @@
     lg_b[...] = jnp.zeros_like(lg_b)
     igp_b[...] = jnp.zeros_like(igp_b)
 
-    x_item.wait_recv()
     for n in range(2):
+        x_items[n].wait_recv()
         hop(0, 1, 1, n).start()
         hop(1, 1, 1, n).start()
-    q_x.wait_recv()
-    q_f.start()
+    for n in range(2):
+        q_xs[n].wait_recv()
+        q_fs[n].start()
     arrive(1, (0,))
 
     lane = lax.broadcasted_iota(jnp.int32, (UB, CH), 1)
@@ -145,7 +153,8 @@
         jnp.concatenate([ugall[0, 4:5, :], ugall[1, 4:5, :]], axis=1), (8, US)
     )
     q_c.wait_recv()
-    q_f.wait_recv()
+    for copy in q_fs:
+        copy.wait_recv()
     for h in range(2):
         mask_users(1 - c, h)
 
@@ -294,7 +303,7 @@
             dev(z + 2 * dr - 1, c, h),
         )
 
-    def matmuls(o, lg, igp, r):
+    def matmuls(o, lg, igp, ib, gacc, r):
         both = jnp.dot(
             lg[pl.ds(pl.multiple_of(r * 2 * CH, 2 * CH), 2 * CH), :], qpair[r], preferred_element_type=F32
         )
@@ -315,19 +324,19 @@
             ones, lo, NT, preferred_element_type=F32
         )
 
-    def item_sum(h):
+    def item_sum(ib, h):
         return jnp.concatenate([ib[2 * h], ib[2 * h + 1]], axis=1)
 
-    def gate_sum():
+    def gate_sum(gacc):
         return jnp.concatenate([gacc[i, 0:2, :] for i in range(4)], axis=0)
 
     def four(v):
         return jnp.concatenate([v] * (BROWS // 8), axis=0)
 
-    def chunk(o, logit, s, lg, igp, o_before, lg_before, igp_before):
+    def chunk(o, logit, s, lg, igp, o_before, lg_before, igp_before, ib, gacc):
         def rows_of(r, carry):
             rows = pl.ds(pl.multiple_of(r * BROWS, BROWS), BROWS)
-            matmuls(o_before, lg_before, igp_before, r)
+            matmuls(o_before, lg_before, igp_before, ib, gacc, r)
             sc = score[o, rows, :]
             soft = jnp.exp2(sc * four(scale2) - four(ltb[...]))
             soft = jnp.where(is_positive(o, r, BROWS), soft - 1.0, soft) * four(inv_t)
@@ -348,100 +357,109 @@
 
         lax.fori_loop(0, CH // BROWS, rows_of, 0, unroll=True)
 
-    def send(dr, jj):
-        @pl.when(jj == 1)
-        def _():
+    def send(dr, d, ib, gacc):
+        if d == 3:
             for h in range(2):
-                sbuf[dr, 2, h] = item_sum(h).astype(BF16)
+                sbuf[dr, 2, h] = item_sum(ib, h).astype(BF16)
                 rs_copy(dr, 3, h).start()
-            gsend[dr, 2] = gate_sum()
+            gsend[dr, 2] = gate_sum(gacc)
             gate_copy(dr, 3).start()
-
-        @pl.when(jj == 2)
-        def _():
+        elif d == 2:
             for h in range(2):
                 rs_copy(dr, 3, h).wait_recv()
-                value = item_sum(h) + rbuf[dr, 2, h].astype(F32)
+                value = item_sum(ib, h) + rbuf[dr, 2, h].astype(F32)
                 if h == dr:
                     rs_copy(dr, 4, h).wait_recv()
                     value = value + rbuf[dr, 3, h].astype(F32)
                 sbuf[dr, 1, h] = value.astype(BF16)
                 rs_copy(dr, 2, h).start()
             gate_copy(dr, 3).wait_recv()
-            value = gate_sum() + grecv[dr, 2]
+            value = gate_sum(gacc) + grecv[dr, 2]
             if dr == 0:
                 gate_copy(0, 4).wait_recv()
                 value = value + grecv[0, 3]
             gsend[dr, 1] = value
             gate_copy(dr, 2).start()
-
-        @pl.when(jj == 3)
-        def _():
+        else:
             for h in range(2):
                 rs_copy(dr, 2, h).wait_recv()
-                sbuf[dr, 0, h] = (item_sum(h) + rbuf[dr, 1, h].astype(F32)).astype(BF16)
+                sbuf[dr, 0, h] = (item_sum(ib, h) + rbuf[dr, 1, h].astype(F32)).astype(BF16)
             for w in (1, 0):
                 last_copy(dr, w).start()
             gate_copy(dr, 2).wait_recv()
-            gsend[dr, 0] = gate_sum() + grecv[dr, 1]
+            gsend[dr, 0] = gate_sum(gacc) + grecv[dr, 1]
             gate_copy(dr, 1).start()
 
     def backward(jj, carry):
         d = 4 - jj
         right = lax.rem(z + d, NZ)
-        chunk(right, logit_b, d - 1, lg_a, igp_a, lax.rem(z + NZ - d, NZ), lg_b, igp_b)
-        send(0, jj)
-        chunk(lax.rem(z + NZ - (d - 1), NZ), logit_a, d - 1, lg_b, igp_b, right, lg_a, igp_a)
-
-        @pl.when(jj == 0)
+        chunk(
+            right, logit_b, d - 1, lg_a, igp_a, lax.rem(z + NZ - d, NZ), lg_b, igp_b, ib_a, gacc_a
+        )
+        for dd in (3, 2):
+
+            @pl.when(d == dd)
+            def _():
+                send(0, dd, ib_a, gacc_a)
+
+        left = lax.rem(z + NZ - (d - 1), NZ)
+        chunk(left, logit_a, d - 1, lg_b, igp_b, right, lg_a, igp_a, ib_b, gacc_b)
+
+        @pl.when(d == 4)
         def _():
             for h in range(2):
-                sbuf[h, 3, h] = item_sum(h).astype(BF16)
+                sbuf[h, 3, h] = item_sum(ib_b, h).astype(BF16)
                 rs_copy(h, 4, h).start()
-            gsend[0, 3] = gate_sum()
+            gsend[0, 3] = gate_sum(gacc_b)
             gate_copy(0, 4).start()
 
-        send(1, jj)
+        for dd in (3, 2):
+
+            @pl.when(d == dd)
+            def _():
+                send(1, dd, ib_b, gacc_b)
+
         return carry
 
     lax.fori_loop(0, NZ // 2, backward, 0)
-
+    send(0, 1, ib_a, gacc_a)
+
+    def u_core(hh, p):
+        h = 1 - x if hh == 0 else x
+        at = pl.ds(pl.multiple_of(h * UB + p * CH, CH), CH)
+        return rc(uacc.at[1 - c, at, :], urecv.at[hh, p], uc_s.at[hh, p], uc_r.at[hh, p], cp)
+
+    def u_x(p):
+        return rc(usend.at[p], uxrecv.at[p], ux_s.at[p], ux_r.at[p], xp)
+
+    def core_sum(hh, p):
+        h = 1 - x if hh == 0 else x
+        at = pl.ds(pl.multiple_of(h * UB + p * CH, CH), CH)
+        u_core(hh, p).wait_recv()
+        return uacc[c, at, :] + urecv[hh, p]
+
+    for hh in range(2):
+        for p in range(2):
+            h = 1 - x if hh == 0 else x
+            matmuls(z, lg_b, igp_b, ib_c, gacc_c, 2 * h + p)
+            u_core(hh, p).start()
+    send(1, 1, ib_b, gacc_b)
+    for p in range(2):
+        usend[p] = core_sum(0, p).astype(BF16)
+        u_x(p).start()
+
+    sums = [item_sum(ib_c, h) for h in range(2)]
+    first = jnp.broadcast_to(x, (CH, UB)) == 0
+    isend[...] = jnp.where(first, sums[1], sums[0]).astype(BF16)
+    keep = jnp.where(first, sums[0], sums[1])
+    i_x = rc(isend, irecv, fx_s.at[0], fx_r.at[0], xp)
+    i_x.start()
     for k in range(K):
         ugsend[k : k + 1, :] = jnp.sum(ugv[k], axis=0, keepdims=True)
     ug_sends = [rc(ugsend, ugrecv.at[i], ugs_s.at[i], ugs_r.at[i], quad[i]) for i in range(3)]
     for s in ug_sends:
         s.start()
-
-    def u_core(hh, p):
-        h = 1 - x if hh == 0 else x
-        at = pl.ds(pl.multiple_of(h * UB + p * CH, CH), CH)
-        return rc(uacc.at[1 - c, at, :], urecv.at[hh, p], uc_s.at[hh, p], uc_r.at[hh, p], cp)
-
-    def u_x(p):
-        return rc(usend.at[p], uxrecv.at[p], ux_s.at[p], ux_r.at[p], xp)
-
-    def core_sum(hh, p):
-        h = 1 - x if hh == 0 else x
-        at = pl.ds(pl.multiple_of(h * UB + p * CH, CH), CH)
-        u_core(hh, p).wait_recv()
-        return uacc[c, at, :] + urecv[hh, p]
-
-    for hh in range(2):
-        for p in range(2):
-            h = 1 - x if hh == 0 else x
-            matmuls(z, lg_b, igp_b, 2 * h + p)
-            u_core(hh, p).start()
-    for p in range(2):
-        usend[p] = core_sum(0, p).astype(BF16)
-        u_x(p).start()
-
-    sums = [item_sum(h) for h in range(2)]
-    first = jnp.broadcast_to(x, (CH, UB)) == 0
-    isend[...] = jnp.where(first, sums[1], sums[0]).astype(BF16)
-    keep = jnp.where(first, sums[0], sums[1])
-    i_x = rc(isend, irecv, fx_s.at[0], fx_r.at[0], xp)
-    i_x.start()
-    gate = gate_sum()
+    gate = gate_sum(gacc_c)
     for dr in range(2):
         gate_copy(dr, 1).wait_recv()
         gate = gate + grecv[dr, 0]
@@ -476,7 +494,7 @@
         at = slice(p * CH, (p + 1) * CH)
         ug_ref[:, at] = (ukeep[at, :] + uxrecv[p].astype(F32)).T
 
-    for s in (x_item, q_x, q_c, q_f, *u_sends, *st_sends, i_x, ig_x, *ug_sends):
+    for s in (*x_items, *q_xs, q_c, *q_fs, *u_sends, *st_sends, i_x, ig_x, *ug_sends):
         s.wait_send()
     for p in range(2):
         u_x(p).wait_send()
@@ -497,14 +515,23 @@
                     hop(dr, s, hh, n).wait_send()
 
 
-def write_out(loss, ug, ig, ugate, igate, *outs):
-    for a, o in zip((loss, ug, ig, ugate, igate), outs):
-        o[...] = a[...]
+def write_out(*refs):
+    ins, outs, held, in_sem, out_sem = refs[:5], refs[5:10], refs[10:15], refs[15], refs[16]
+    come = [pltpu.make_async_copy(ins[i], held[i], in_sem.at[i]) for i in range(5)]
+    leave = [pltpu.make_async_copy(held[i], outs[i], out_sem.at[i]) for i in range(5)]
+    for i in (1, 2, 0, 3, 4):
+        come[i].start()
+    for i in (1, 2, 0, 3, 4):
+        come[i].wait()
+        leave[i].start()
+    for copy in leave:
+        copy.wait()
 
 
 def body(query, candidate, query_gate, candidate_gate, slope, scale, target):
     vmem = pl.BlockSpec(memory_space=pltpu.VMEM)
     smem = pl.BlockSpec(memory_space=pltpu.SMEM)
+    hbm = pl.BlockSpec(memory_space=pl.ANY)
     dma = pltpu.SemaphoreType.DMA
     scratch = [
         pltpu.VMEM((2, 2, UB, UB), BF16),
@@ -534,8 +561,12 @@
         pltpu.VMEM((4, CH, 2 * CH), F32),
         pltpu.VMEM((4, CH, 2 * CH), F32),
         pltpu.VMEM((4, 8, CH), F32),
+        pltpu.VMEM((4, 8, CH), F32),
+        pltpu.VMEM((4, 8, CH), F32),
         pltpu.VMEM((K, 8, US), F32),
         pltpu.VMEM((2, US, UB), F32),
+        pltpu.VMEM((4, CH, CH), F32),
+        pltpu.VMEM((4, CH, CH), F32),
         pltpu.VMEM((4, CH, CH), F32),
         pltpu.VMEM((4, US, CH), BF16),
         pltpu.VMEM((2, 4, 2, CH, UB), BF16),
@@ -551,8 +582,8 @@
         pltpu.VMEM((2, K, CH), F32),
         pltpu.VMEM((K, US), F32),
         pltpu.VMEM((3, K, US), F32),
-        dma((1,)), dma((1,)),
-        dma((3,)), dma((3,)),
+        dma((2,)), dma((2,)),
+        dma((5,)), dma((5,)),
         dma((3,)), dma((3,)),
         dma((2, 4, 2, 2)), dma((2, 4, 2, 2)),
         dma((3,)), dma((3,)),
@@ -581,7 +612,11 @@
         ),
     )(query, candidate, query_gate, candidate_gate, slope, scale, target.reshape(1, UB))
     loss, ug, ig, ugate, igate = pl.pallas_call(
-        write_out, out_shape=outs, in_specs=[vmem] * 5, out_specs=(vmem,) * 5
+        write_out,
+        out_shape=outs,
+        in_specs=[hbm] * 5,
+        out_specs=(hbm,) * 5,
+        scratch_shapes=[*(pltpu.VMEM(out.shape, F32) for out in outs), dma((5,)), dma((5,))],
     )(*results)
     return loss.reshape(UB), ug, ig, ugate, igate
 

time: 66 us -> 65.9 us (level)
  no operation moved by 1% of the time
where the time goes in v6:
time: 65.9 us; the launch traced here: 65.8 us
  Pallas kernels  64.5 us (98%)
  between operations  1.29 us (2%)
    pallas_call x1, Pallas kernels, body(): pl.pallas_call(kernel, out_shape=outs, in_specs=[vmem, vmem, vmem, vmem,...  62.7 us
    pallas_call x1, Pallas kernels, body(): pl.pallas_call(write_out, out_shape=outs, in_specs=[hbm] * 5, out_specs=(...  1.83 us

profile of v6, /device:TPU:1, one launch (start us, length us, event | category | flops | bytes accessed | tf_op | source)
XLA Modules:
  0.0 65.8 jit_solution(15636628692197216918)
XLA Ops:
  1.3 62.7 %shard_map.110 = (f32[1,256]{1,0:T(1,128)}, f32[256,256]{1,0:T(8,128)}, f32[256,256]{1,0:T(8,128)}, f32[4,256]{1,0:T(4,128)}, f32[4,256]{1,0:T(4,128)}) custom-call(bf16[256,256]{1,0:T(8,128)(2,1)} %q_ref.1, bf16[256,256]{1,0:T(8,128)(2,1)} %c_ref.1, bf16[4,256]{1,0:T(4,128)(2,1)} %gq_ref.1, bf16[4,256]{1,0:T(4,128)(2,1)} %gc_ref.1, f32[8]{0:T(128)} %slope_ref.1, ...), custom_call_target="tpu_custom_call" | custom-call | tf_op jit(solution)/shard_map/pallas_call | solution.py:604
  64.0 1.8 %shard_map.111 = (f32[1,256]{1,0:T(1,128)}, f32[256,256]{1,0:T(8,128)}, f32[256,256]{1,0:T(8,128)}, f32[4,256]{1,0:T(4,128)}, f32[4,256]{1,0:T(4,128)}) custom-call(f32[1,256]{1,0:T(1,128)} %get-tuple-element.15.refs_0_, f32[256,256]{1,0:T(8,128)} %get-tuple-element.16.refs_1_, f32[256,256]{1,0:T(8,128)} %get-tuple-element.17.refs_2_, ...), custom_call_target="tpu_custom_call" | custom-call | tf_op jit(solution)/shard_map/pallas_call | solution.py:614

commit v7 on v4

--- a/solution.py
+++ b/solution.py
@@ -13,7 +13,7 @@
 US = 512
 CH = 128
 SLOT = CH + 16
-PIECES = ((0, 80), (80, 64))
+PIECES = (((0, 64), (64, 64)), ((0, 80), (80, 64)))
 K = 8
 ROWS = 16
 BROWS = 32
@@ -59,10 +59,9 @@
     gc = jnp.concatenate([gc, gc], axis=0)
     low = jnp.broadcast_to(x, (16, CH)) == 0
     blank = jnp.zeros((16, CH), F32)
-    own_gate = jnp.concatenate([jnp.where(low, gc[:, :CH], gc[:, CH:]), blank], axis=1)
+    own_gate = jnp.where(low, gc[:, :CH], gc[:, CH:]).astype(BF16)
     peer_gate = jnp.concatenate([jnp.where(low, gc[:, CH:], gc[:, :CH]), blank], axis=1)
     call[z, x, :CH, :] = c_ref[own_rows, :]
-    call[z, x, CH:, :] = own_gate.astype(BF16)
     xstage[:CH, :] = c_ref[peer_rows, :]
     xstage[CH:, :] = peer_gate.astype(BF16)
     qall[c, x] = q_ref[...]
@@ -75,7 +74,7 @@
         step = 1 - 2 * dr
         o = lax.rem(z - step * min(s - 1, 2) + NZ, NZ)
         h = x if hh == 0 else 1 - x
-        at = call.at[o, h, pl.ds(*PIECES[n]), :]
+        at = call.at[o, h, pl.ds(*PIECES[hh][n]), :]
         return rc(at, at, ag_s.at[dr, s - 1, hh, n], ag_r.at[dr, s - 1, hh, n],
                   dev(z + (2 * step if s == 4 else step), c, x))
 
@@ -115,6 +114,7 @@
     igp_b[...] = jnp.zeros_like(igp_b)
 
     x_item.wait_recv()
+    call[z, 1 - x, CH:, CH:] = own_gate
     for n in range(2):
         hop(0, 1, 1, n).start()
         hop(1, 1, 1, n).start()
@@ -162,8 +162,9 @@
         return jnp.concatenate([tgtb[...]] * (rows // 8), axis=0) == ids.astype(F32)
 
     def gates_of(o, gpad, git):
-        gpad[0:16, :] = call[o, 0, CH:, :CH].astype(F32)
-        gpad[16:32, :] = call[o, 1, CH:, :CH].astype(F32)
+        gates = call[o, 1 - x, CH:, :].astype(F32)
+        gpad[pl.ds(pl.multiple_of((1 - x) * 16, 16), 16), :] = gates[:, :CH]
+        gpad[pl.ds(pl.multiple_of(x * 16, 16), 16), :] = gates[:, CH:]
         git[...] = gpad[...].T * LOG2E
 
     def logits_of(o, logit, s, k):

time: 66 us -> 66.1 us (level)
  no operation moved by 1% of the time
where the time goes in v7:
time: 66.1 us; the launch traced here: 66 us
  Pallas kernels  64.7 us (98%)
  between operations  1.29 us (2%)
    pallas_call x1, Pallas kernels, body(): pl.pallas_call(kernel, out_shape=outs, in_specs=[vmem, vmem, vmem, vmem,...  62.8 us
    pallas_call x1, Pallas kernels, body(): pl.pallas_call(write_out, out_shape=outs, in_specs=[vmem] * 5, out_specs=...  1.86 us

profile of v7, /device:TPU:1, one launch (start us, length us, event | category | flops | bytes accessed | tf_op | source)
XLA Modules:
  0.0 66.0 jit_solution(5245881300432530742)
XLA Ops:
  1.3 62.8 %shard_map.110 = (f32[1,256]{1,0:T(1,128)}, f32[256,256]{1,0:T(8,128)}, f32[256,256]{1,0:T(8,128)}, f32[4,256]{1,0:T(4,128)}, f32[4,256]{1,0:T(4,128)}) custom-call(bf16[256,256]{1,0:T(8,128)(2,1)} %q_ref.1, bf16[256,256]{1,0:T(8,128)(2,1)} %c_ref.1, bf16[4,256]{1,0:T(4,128)(2,1)} %gq_ref.1, bf16[4,256]{1,0:T(4,128)(2,1)} %gc_ref.1, f32[8]{0:T(128)} %slope_ref.1, ...), custom_call_target="tpu_custom_call" | custom-call | tf_op jit(solution)/shard_map/pallas_call | solution.py:574
  64.1 1.9 %shard_map.111 = (f32[1,256]{1,0:T(1,128)}, f32[256,256]{1,0:T(8,128)}, f32[256,256]{1,0:T(8,128)}, f32[4,256]{1,0:T(4,128)}, f32[4,256]{1,0:T(4,128)}) custom-call(f32[1,256]{1,0:T(1,128)} %get-tuple-element.15.loss, f32[256,256]{1,0:T(8,128)} %get-tuple-element.16.ug, f32[256,256]{1,0:T(8,128)} %get-tuple-element.17.ig, f32[4,256]{1,0:T(4,128)} %get-tuple-element.18.ugate, ...), custom_call_target="tpu_custom_call" | custom-call | tf_op jit(solution)/shard_map/pallas_call | solution.py:584
